TPU v7x, 512 devices: a whole 4x4x16 slice. The times are simulated.
512 devices in a mesh: dp: 64 (over x_hi, z, core), mp: 8 (over y, x_lo).
Axes of the slice: x: 4 (x_hi: 2, x_lo: 2; x = x_hi * 2 + x_lo), y: 4, z: 16, core: 2. Of those that a mesh axis runs over, the one named last changes fastest.
Arguments:
- patches: bfloat16 [32768, 1152], P('dp', 'mp'), may hold values from -6 to 6
- patch_shard: int32 [32768, 1], P('dp'), may hold values from 0 to 63; in each aligned block of 512 rows (0 to 511, 512 to 1023, ...) at most 10 rows name the same one
- patch_image: int32 [64, 512], P('dp'), may hold values from 0 to 15, as said below
- caption_of: int32 [1024], P('dp'), may hold values from 0 to 1023, as said below
- text_embed: bfloat16 [1024, 1152], P('dp', 'mp'), may hold values from -8 to 8
- ln_gain: bfloat16 [1152], P('mp'), may hold values from 0.099609375 to 1.8984375
- fc1_weight: bfloat16 [1152, 4304], P(None, 'mp'), may hold values from -0.1875 to 0.1875
- fc1_bias: bfloat16 [4304], P('mp'), may hold values from -3 to 3
- fc2_weight: bfloat16 [4304, 1152], P('mp'), may hold values from -0.09375 to 0.09375
- fc2_bias: bfloat16 [1152], P('mp'), may hold values from -3 to 3
Outputs:
- packed: bfloat16 [64, 640, 1152], P('dp', None, 'mp')
- image_grad: float32 [1024, 1152], P('dp', 'mp')
- text_grad: float32 [1024, 1152], P('dp', 'mp')
Inputs may be any that keep to these rules, and one draw needn't show every extreme that they name: `patch_shard`: within the 512 rows of one dp shard at most 10 rows name the same encoder shard, and in some dp shard one encoder shard is named by exactly 10 rows. `patch_image`: in each dp shard the ids never fall and every image 0 to 15 has one or more patches; no image has more than 64 patches and some image has exactly 64. `caption_of`: each text is paired with exactly one image.
All inputs are finite; a program needn't handle non-finite values.
Results may differ from a plain program's by a relative error of at most 0.017.
Values may be sent and summed in bfloat16 or wider, within the bound.
A program may use at most 128 MiB of HBM per device.

v0:
```python
import jax
import jax.numpy as jnp
from jax import lax
from jax.sharding import PartitionSpec as P

LOGIT_SCALE = 10.0
LOGIT_BIAS = -2.0


def shifted(value, axis, steps):
    count = lax.axis_size(axis)
    pairs = [(source, (source + steps) % count) for source in range(count)]
    return lax.ppermute(value, axis, pairs)


def layer_norm(row_block, row_gain):
    widened = row_block.astype(jnp.float32)
    centre = widened - jnp.mean(widened, axis=-1, keepdims=True)
    spread = jnp.mean(centre * centre, axis=-1, keepdims=True)
    return (centre * lax.rsqrt(spread + 1e-06) * row_gain.astype(jnp.float32)).astype(jnp.bfloat16)


def unit_rows(widened):
    return (widened * lax.rsqrt(jnp.sum(widened * widened, axis=-1, keepdims=True) + 1e-06)).astype(
        jnp.bfloat16
    )


def hidden_units(normed, fc1_weight, fc1_bias):
    return jax.nn.gelu(
        jnp.dot(normed, fc1_weight, preferred_element_type=jnp.float32)
        + fc1_bias.astype(jnp.float32),
        approximate=True,
    ).astype(jnp.bfloat16)


def slot_ranks(targets, shard_count):
    shard_ids = jnp.arange(shard_count, dtype=jnp.int32)
    member = (targets[:, None] == shard_ids[None, :]).astype(jnp.int32)
    before = jnp.cumsum(member, axis=0) - member
    return jnp.sum(before * member, axis=1)


def encode_block(row_block, params):
    ln_gain, fc1_weight, fc1_bias, fc2_weight, fc2_bias = params
    full_block, full_gain = (
        lax.all_gather(row_block, "mp", axis=1, tiled=True),
        lax.all_gather(ln_gain, "mp", axis=0, tiled=True),
    )
    hidden = hidden_units(layer_norm(full_block, full_gain), fc1_weight, fc1_bias)
    partial_out = jnp.dot(hidden, fc2_weight, preferred_element_type=jnp.float32)
    mixed_sum = lax.psum_scatter(partial_out, "mp", scatter_dimension=1, tiled=True)
    return (row_block.astype(jnp.float32) + mixed_sum + fc2_bias.astype(jnp.float32)).astype(
        jnp.bfloat16
    )


def shards(
    patches,
    patch_shard,
    patch_image,
    caption_of,
    text_embed,
    ln_gain,
    fc1_weight,
    fc1_bias,
    fc2_weight,
    fc2_bias,
):
    dp_count = lax.axis_size("dp")
    feature_part = patches.shape[1]
    row_count = patches.shape[0]
    capacity = max(2, 5 * row_count // (4 * dp_count))
    params = (ln_gain, fc1_weight, fc1_bias, fc2_weight, fc2_bias)
    targets = patch_shard[:, 0]
    slot_index = targets * capacity + slot_ranks(targets, dp_count)
    outgoing = (
        jnp.zeros((dp_count * capacity, feature_part), jnp.bfloat16).at[slot_index].set(patches)
    )
    outgoing = outgoing.reshape(dp_count, capacity, feature_part)
    received = lax.all_to_all(outgoing, "dp", split_axis=0, concat_axis=0, tiled=True)
    slot_count = received.shape[1]
    coded = encode_block(received.reshape(-1, feature_part), params)
    coded = coded.reshape(dp_count, slot_count, feature_part)
    returned = lax.all_to_all(coded, "dp", split_axis=0, concat_axis=0, tiled=True)
    coded, returned = (coded, returned)
    packed = coded.reshape(1, dp_count * capacity, feature_part)
    encoded = returned.reshape(-1, feature_part)[slot_index]
    image_count = caption_of.shape[0]
    image_ids = jnp.arange(image_count, dtype=jnp.int32)
    member = patch_image[0][None, :] == image_ids[:, None]
    row_sums = jnp.dot(member.astype(jnp.bfloat16), encoded, preferred_element_type=jnp.float32)
    counts = jnp.sum(member.astype(jnp.float32), axis=1, keepdims=True)
    pooled = lax.all_gather(row_sums / counts, "mp", axis=1, tiled=True)
    image_unit = unit_rows(pooled)
    text_rows = lax.all_to_all(text_embed, "mp", split_axis=0, concat_axis=1, tiled=True)
    text_unit = unit_rows(text_rows.astype(jnp.float32))
    text_count = text_unit.shape[0]
    full_width = text_unit.shape[1]
    shard_here = lax.axis_index("dp")
    member_here = lax.axis_index("mp")
    offsets = jnp.arange(text_count, dtype=jnp.int32)

    def score(text_block, anchor):
        leading = anchor % dp_count * image_count + member_here * text_count
        logits = (
            LOGIT_SCALE
            * jnp.einsum("id,jd->ij", image_unit, text_block, preferred_element_type=jnp.float32)
            + LOGIT_BIAS
        )
        paired = (caption_of[:, None] == (leading + offsets)[None, :]).astype(jnp.float32)
        pair_coef = (jax.nn.sigmoid(logits) - paired).astype(jnp.bfloat16)
        to_images = LOGIT_SCALE * jnp.dot(pair_coef, text_block, preferred_element_type=jnp.float32)
        to_texts = LOGIT_SCALE * jnp.einsum(
            "ij,id->jd", pair_coef, image_unit, preferred_element_type=jnp.float32
        )
        return (to_images, to_texts)

    text_zero = jnp.zeros((text_count, full_width), jnp.float32)
    image_zero = jnp.zeros((image_count, full_width), jnp.float32)

    def forward_turn(hop_index, carry):
        text_block, travel_sum, image_acc = carry
        to_images, to_texts = score(text_block, shard_here - hop_index)
        moved_block = shifted(text_block, "dp", 1)
        travel_sum = shifted(travel_sum + to_texts, "dp", 1)
        return (moved_block, travel_sum, image_acc + to_images)

    final_block, text_acc, image_acc = lax.fori_loop(
        0, dp_count, forward_turn, (text_unit, text_zero, image_zero)
    )
    image_grad = lax.psum_scatter(
        image_acc.astype(jnp.bfloat16), "mp", scatter_dimension=1, tiled=True
    ).astype(jnp.float32)
    text_grad = lax.all_to_all(text_acc, "mp", split_axis=1, concat_axis=0, tiled=True)
    return (packed, image_grad, text_grad)


def solution(mesh):
    return jax.shard_map(
        shards,
        mesh=mesh,
        in_specs=(
            P("dp", "mp"),
            P("dp", None),
            P("dp", None),
            P("dp"),
            P("dp", "mp"),
            P("mp"),
            P(None, "mp"),
            P("mp"),
            P("mp", None),
            P("mp"),
        ),
        out_specs=(P("dp", None, "mp"), P("dp", "mp"), P("dp", "mp")),
        check_vma=False,
    )
```

profile of v0, /device:TPU:1, one launch (start us, length us, event | category | flops | bytes accessed | tf_op | source)
XLA Modules:
  0.0 979.3 jit_solution(8142567442424618340)
XLA Ops:
  15.1 40.6 %all_to_all.42 = bf16[64,2,720]{2,1,0:T(2,128)(2,1)S(1)} all-to-all(bf16[64,2,720]{2,1,0:T(2,128)(2,1)S(1)} %reshape.112), channel_id=1, replica_groups=mesh['dp'=64,'mp'=8] {'dp'}, dimensions={0} | all-to-all | bytes 368640 | tf_op jit(solution)/shard_map/all_to_all | solution.py:81
  59.5 16.2 %all-reduce = bf16[1152]{0:T(1024)(128)(2,1)S(1)} all-reduce(bf16[1152]{0:T(1024)(128)(2,1)S(1)} %dynamic-update-slice), channel_id=1, replica_groups=mesh['dp'=64,'mp'=8] {'mp'}, use_global_device_ids=true, to_apply=%add | all-reduce | flops 1152 | bytes 4608
  75.8 18.7 %all-gather.3.cloned.1.call-done = bf16[640,1152]{0,1:T(8,128)(2,1)} async-done(((bf16[640,144]{0,1:T(8,128)(2,1)}), bf16[640,1152]{0,1:T(8,128)(2,1)}) %all-gather.3.cloned.1.call-update) | async-done | bytes 1474576 | tf_op jit(solution)/shard_map/all_gather | solution.py:47
  96.7 6.1 fusion.33
  107.7 4.8 all-to-all-done.1
  112.5 68.5 %reduce-scatter.5.cloned.1.call-done = f32[640,144]{0,1:T(8,128)} async-done(((f32[640,1152]{0,1:T(8,128)}), f32[640,144]{0,1:T(8,128)}) %reduce-scatter.5.cloned.1.call-update) | async-done | bytes 368656 | tf_op jit(solution)/shard_map/reduce_scatter | solution.py:52
  183.6 15.7 %all-to-all-start.2 = ((bf16[64,2,720]{2,1,0:T(2,128)(2,1)}), bf16[64,2,720]{2,1,0:T(2,128)(2,1)S(1)}, u32[]{:S(2)}, u32[]{:S(2)}) async-start(bf16[64,2,720]{2,1,0:T(2,128)(2,1)} %reshape.114), calls=%async_computation.3 | async-start | bytes 393216 | tf_op jit(solution)/shard_map/all_to_all | solution.py:85
  199.8 20.6 %all-to-all-done.2 = bf16[64,2,720]{2,1,0:T(2,128)(2,1)S(1)} async-done(((bf16[64,2,720]{2,1,0:T(2,128)(2,1)}), bf16[64,2,720]{2,1,0:T(2,128)(2,1)S(1)}, u32[]{:S(2)}, u32[]{:S(2)}) %all-to-all-start.2) | async-done | bytes 184352 | tf_op jit(solution)/shard_map/all_to_all | solution.py:85
  223.3 22.3 %all-gather = f32[8,144,16]{1,2,0:T(8,128)S(1)} all-gather(f32[1,144,16]{1,2,0:T(8,128)S(1)} %fusion.31), channel_id=1, replica_groups=mesh['dp'=64,'mp'=8] {'mp'}, dimensions={0}, use_global_device_ids=true | all-gather | bytes 82944 | tf_op jit(solution)/shard_map/all_gather | solution.py:94
  246.1 692.2 %while.20 = (s32[]{:T(128)}, bf16[2,1152]{1,0:T(2,128)(2,1)S(1)}, f32[2,1152]{1,0:T(2,128)S(1)}, f32[16,1152]{1,0:T(8,128)S(1)}, bf16[16,1152]{1,0:T(8,128)(2,1)...) while((s32[]{:T(128)}, bf16[2,1152]{1,0:T(2,128)(2,1)S(1)}, ...), condition=%wide.region_11.12_spmd.clone, body=%wide.region_10.11_spmd.clone.sunk | while | flops 281395 | bytes 313980 | solution.py:129
  246.1 8.9 collective-permute-start
  271.9 4.2 collective-permute-done
  282.7 4.2 collective-permute-done
  293.5 4.2 collective-permute-done
  304.4 4.2 collective-permute-done
  315.2 4.2 collective-permute-done
  326.0 4.2 collective-permute-done
  336.8 4.2 collective-permute-done
  347.6 4.2 collective-permute-done
  358.5 4.2 collective-permute-done
  369.3 4.2 collective-permute-done
  380.1 4.2 collective-permute-done
  390.9 4.2 collective-permute-done
  401.7 4.2 collective-permute-done
  412.5 4.2 collective-permute-done
  423.4 4.2 collective-permute-done
  434.2 4.2 collective-permute-done
  445.0 4.2 collective-permute-done
  455.8 4.2 collective-permute-done
  466.6 4.2 collective-permute-done
  477.5 4.2 collective-permute-done
  488.3 4.2 collective-permute-done
  499.1 4.2 collective-permute-done
  509.9 4.2 collective-permute-done
  520.7 4.2 collective-permute-done
  531.5 4.2 collective-permute-done
  542.4 4.2 collective-permute-done
  553.2 4.2 collective-permute-done
  564.0 4.2 collective-permute-done
  574.8 4.2 collective-permute-done
  585.6 4.2 collective-permute-done
  596.5 4.2 collective-permute-done
  607.3 4.2 collective-permute-done
  618.1 4.2 collective-permute-done
  628.9 4.2 collective-permute-done
  639.7 4.2 collective-permute-done
  650.5 4.2 collective-permute-done
  661.4 4.2 collective-permute-done
  672.2 4.2 collective-permute-done
  683.0 4.2 collective-permute-done
  693.8 4.2 collective-permute-done
  704.6 4.2 collective-permute-done
  715.4 4.2 collective-permute-done
  726.3 4.2 collective-permute-done
  737.1 4.2 collective-permute-done
  747.9 4.2 collective-permute-done
  758.7 4.2 collective-permute-done
  769.5 4.2 collective-permute-done
  780.4 4.2 collective-permute-done
  812.8 4.2 collective-permute-done
  888.5 4.2 collective-permute-done
  931.8 4.2 collective-permute-done
  939.3 7.4 all_to_all.43
  947.3 24.0 %reduce-scatter.7.cloned.1.call-done = bf16[144,16]{1,0:T(8,128)(2,1)} async-done(((bf16[1152,16]{1,0:T(8,128)(2,1)}), bf16[144,16]{1,0:T(8,128)(2,1)}) %reduce-scatter.7.cloned.1.call-update) | async-done | bytes 4624
  (606 shorter events, 491.7 us)
Async XLA Ops:
  7.2 87.3 %all-gather.3.cloned.1.call-start = ((), (), s32[]{:S(2)}) async-start(), calls=%async_computation.6 | async-start | bytes 1658880 | tf_op jit(solution)/shard_map/all_gather | solution.py:47
  57.3 123.7 %reduce-scatter.5.cloned.1.call-start = ((), (), s32[]{:S(2)}) async-start(), calls=%async_computation.7 | async-start | bytes 3317760 | tf_op jit(solution)/shard_map/reduce_scatter | solution.py:52
  183.6 36.9 %all-to-all-start.2 = ((bf16[64,2,720]{2,1,0:T(2,128)(2,1)}), bf16[64,2,720]{2,1,0:T(2,128)(2,1)S(1)}, u32[]{:S(2)}, u32[]{:S(2)}) async-start(bf16[64,2,720]{2,1,0:T(2,128)(2,1)} %reshape.114), calls=%async_computation.3 | async-start | bytes 393216 | tf_op jit(solution)/shard_map/all_to_all | solution.py:85
  199.3 772.0 %reduce-scatter.7.cloned.1.call-start = ((), (), s32[]{:S(2)}) async-start(), calls=%async_computation.8 | async-start | bytes 331776
  246.1 11.3 %collective-permute-start = (bf16[2,1152]{1,0:T(2,128)(2,1)S(1)}, bf16[2,1152]{1,0:T(2,128)(2,1)S(1)}, u32[]{:S(2)}, u32[]{:S(2)}) collective-permute-start(bf16[2,1152]{1,0:T(2,128)(2,1)S(1)} %copy.56), channel_id=1, source_target_pairs={{0,8},{8,16},{16,24},{24,32},{32,40},{40,48},{48,56},{56,64},{64,7... | collective-permute-start | bytes 13832 | tf_op jit(solution)/shard_map/while/body/eval_jaxpr/ppermute | solution.py:13
  269.8 8.6 collective-permute-start.1
  280.6 8.6 collective-permute-start.1
  291.4 8.6 collective-permute-start.1
  302.2 8.6 collective-permute-start.1
  313.0 8.6 collective-permute-start.1
  323.9 8.6 collective-permute-start.1
  334.7 8.6 collective-permute-start.1
  345.5 8.6 collective-permute-start.1
  356.3 8.6 collective-permute-start.1
  367.1 8.6 collective-permute-start.1
  377.9 8.6 collective-permute-start.1
  388.8 8.6 collective-permute-start.1
  399.6 8.6 collective-permute-start.1
  410.4 8.6 collective-permute-start.1
  421.2 8.6 collective-permute-start.1
  432.0 8.6 collective-permute-start.1
  442.9 8.6 collective-permute-start.1
  453.7 8.6 collective-permute-start.1
  464.5 8.6 collective-permute-start.1
  475.3 8.6 collective-permute-start.1
  486.1 8.6 collective-permute-start.1
  496.9 8.6 collective-permute-start.1
  507.8 8.6 collective-permute-start.1
  518.6 8.6 collective-permute-start.1
  529.4 8.6 collective-permute-start.1
  540.2 8.6 collective-permute-start.1
  551.0 8.6 collective-permute-start.1
  561.9 8.6 collective-permute-start.1
  572.7 8.6 collective-permute-start.1
  583.5 8.6 collective-permute-start.1
  594.3 8.6 collective-permute-start.1
  605.1 8.6 collective-permute-start.1
  615.9 8.6 collective-permute-start.1
  626.8 8.6 collective-permute-start.1
  637.6 8.6 collective-permute-start.1
  648.4 8.6 collective-permute-start.1
  659.2 8.6 collective-permute-start.1
  670.0 8.6 collective-permute-start.1
  680.8 8.6 collective-permute-start.1
  691.7 8.6 collective-permute-start.1
  702.5 8.6 collective-permute-start.1
  713.3 8.6 collective-permute-start.1
  724.1 8.6 collective-permute-start.1
  734.9 8.6 collective-permute-start.1
  745.8 8.6 collective-permute-start.1
  756.6 8.6 collective-permute-start.1
  767.4 8.6 collective-permute-start.1
  778.2 8.6 collective-permute-start.1
  789.0 8.6 collective-permute-start.1
  799.8 8.6 collective-permute-start.1
  810.7 8.6 collective-permute-start.1
  821.5 8.6 collective-permute-start.1
  832.3 8.6 collective-permute-start.1
  843.1 8.6 collective-permute-start.1
  853.9 8.6 collective-permute-start.1
  864.8 8.6 collective-permute-start.1
  875.6 8.6 collective-permute-start.1
  886.4 8.6 collective-permute-start.1
  908.0 8.6 collective-permute-start.1
  (79 other events, 929.1 us)
Sparse Core Ops, SparseCore 0:
  57.4 37.0 all-gather.2
  103.0 77.9 reduce-scatter.4
  939.3 31.9 reduce-scatter.6
where the time goes:
time: 988 us; the launch traced here: 979 us
  waiting for transfers between devices  540 us (55%)
  starting transfers between devices  273 us (28%)
  blocking collectives  86.6 us (9%)
  matrix products  36.2 us (4%)
  local copies, waits for them, and re-layouts  16 us (2%)
  between operations  14.7 us (1%)
    ppermute x128, waiting for transfers between devices, shifted(): return lax.ppermute(value, axis, pairs)  404 us
    ppermute x128, starting transfers between devices, shifted(): return lax.ppermute(value, axis, pairs)  254 us
    reduce_scatter x1, waiting for transfers between devices, encode_block(): lax.psum_scatter(partial_out, 'mp', scatter_dimension=1, tiled=True)  68.5 us
    all_to_all x1, blocking collectives, shards(): lax.all_to_all(outgoing, 'dp', split_axis=0, concat_axis=0, tiled=True)  40.6 us
    unnamed x4, waiting for transfers between devices  24 us
    all_gather x1, blocking collectives, shards(): pooled = lax.all_gather(row_sums / counts, 'mp', axis=1, tiled=True)  22.3 us
    all_to_all x1, waiting for transfers between devices, shards(): lax.all_to_all(coded, 'dp', split_axis=0, concat_axis=0, tiled=True)  20.6 us
  transfers between devices with their start and end apart: 133, of which 132 were waited for; matrix products, arithmetic and copies ran while one was open for 3% of the time, Pallas kernels for 0%

commit v1 on v0

v1 whole, which is shorter than its diff:
```python
import functools

import jax
import jax.numpy as jnp
from jax import lax
from jax.experimental import pallas as pl
from jax.experimental.pallas import tpu as pltpu
from jax.sharding import PartitionSpec as P

LOGIT_SCALE = 10.0
LOGIT_BIAS = -2.0
F32 = jnp.float32
BF16 = jnp.bfloat16
I32 = jnp.int32
MESH = pl.DeviceIdType.MESH

DP, MP = 64, 8
GROUP = 8
ROWS, PART, FULL = 512, 144, 1152
FF, FFP = 538, 640
IMG, CAP = 16, 10
SLOTS = DP * CAP
CH = 2
L = ROWS // CH
SIDE = GROUP * IMG
XROWS = PART + 16


def nn(a, b):
    return jnp.dot(a, b, preferred_element_type=F32)


def nt(a, b):
    return lax.dot_general(a, b, (((1,), (1,)), ((), ())), preferred_element_type=F32)


def tn(a, b):
    return lax.dot_general(a, b, (((0,), (0,)), ((), ())), preferred_element_type=F32)


def iota(shape, axis):
    return lax.broadcasted_iota(I32, shape, axis)


def gelu(h):
    return 0.5 * h * (1.0 + jnp.tanh(0.7978845608028654 * (h + 0.044715 * (h * h * h))))


def wide(column_block):
    return jnp.concatenate([column_block] * (L // 128), axis=1)


def kernel(
    x_hbm, text_hbm, target_hbm, owner_hbm, caption_hbm, gain_hbm, b1_hbm, b2_hbm, w1_hbm, w2_hbm,
    packed_ref, image_grad_ref, text_grad_ref,
    x_ref, text_ref, target_ref, owner_ref, caption_ref, gain_ref, b1_ref, b2_ref, w1, w2,
    small_ref, w2t, xall, gain_b, b1_b, b2_b, hid, part_out, part_in,
    pool_out, pool_in, tbuf, ibuf, pair_out, pair_in, coef_in, grad_out, grad_in,
    pick, empty_pick, sel, rows_out, slot_out, slot_in,
    load_sem, x_send, x_recv, t_send, t_recv, p_send, p_recv,
    pool_send, pool_recv, i_send, i_recv, pair_send, pair_recv, coef_send, coef_recv,
    grad_send, grad_recv, slot_send, slot_recv,
):
    s = lax.axis_index("dp")
    m = lax.axis_index("mp")
    a = s // GROUP
    b = lax.rem(s, GROUP)
    neighbour = lax.rem(s + 1, DP)

    ring, side = m // 2, lax.rem(m, 2)
    ahead = lax.rem(ring + 1, 4) * 2 + side
    behind = lax.rem(ring + 3, 4) * 2 + side
    far = lax.rem(ring + 2, 4) * 2 + side
    across = ring * 2 + 1 - side
    ahead_across = lax.rem(ring + 1, 4) * 2 + 1 - side
    behind_across = lax.rem(ring + 3, 4) * 2 + 1 - side
    far_across = lax.rem(ring + 2, 4) * 2 + 1 - side

    loads = [
        pltpu.make_async_copy(src, dst, load_sem.at[n])
        for n, (src, dst) in enumerate(
            (
                (x_hbm, x_ref), (gain_hbm, gain_ref), (text_hbm, text_ref), (caption_hbm, caption_ref),
                (target_hbm, target_ref), (owner_hbm, owner_ref), (b1_hbm, b1_ref), (b2_hbm, b2_ref),
                (w1_hbm, w1), (w2_hbm, w2),
            )
        )
    ]
    for load in loads:
        load.start()

    barrier = pltpu.get_barrier_semaphore()

    def greet_mp(i, c):
        pl.semaphore_signal(barrier, inc=1, device_id=(s, lax.rem(m + i, MP)), device_id_type=MESH)
        return c

    def greet_dp(i, c):
        pl.semaphore_signal(barrier, inc=1, device_id=(lax.rem(s + i, DP), m), device_id_type=MESH)
        return c

    lax.fori_loop(1, MP, greet_mp, 0)
    lax.fori_loop(1, DP, greet_dp, 0)

    def to_member(member, src, dst, send, recv):
        return pltpu.make_async_remote_copy(
            src_ref=src, dst_ref=dst, send_sem=send, recv_sem=recv,
            device_id=(s, member), device_id_type=MESH,
        )

    def to_mp(i, src, dst, send, recv):
        return to_member(lax.rem(m + i, MP), src, dst, send, recv)

    def to_dp(peer, src, dst, send, recv):
        return pltpu.make_async_remote_copy(
            src_ref=src, dst_ref=dst, send_sem=send, recv_sem=recv,
            device_id=(peer, m), device_id_type=MESH,
        )

    small_ref[...] = jnp.zeros_like(small_ref)
    loads[0].wait()
    loads[1].wait()
    small_ref[1:2, 0:PART] = gain_ref[...].astype(F32).reshape(1, PART)
    for c in range(CH):
        xall[c, m, 0:PART] = x_ref[:, c * L : (c + 1) * L]
    xall[0, m, PART:XROWS] = jnp.broadcast_to(small_ref[1:2, 0:L], (XROWS - PART, L)).astype(BF16)

    pl.semaphore_wait(barrier, DP + MP - 2)

    def block(c, member):
        return xall.at[c, member, pl.ds(0, XROWS if c == 0 else PART)]

    def hand_on(c, owner, member, kind):
        to_member(member, block(c, owner), block(c, owner), x_send.at[c], x_recv.at[c, kind]).start()

    def expect(c, kind):
        to_member(across, block(c, m), block(c, m), x_send.at[c], x_recv.at[c, kind]).wait_recv()

    for c in range(CH):
        hand_on(c, m, across, 2)
        hand_on(c, m, ahead, 0)
        hand_on(c, m, behind, 1)

    for load in loads[2:8]:
        load.wait()
    small_ref[0:1, 0:FF] = b1_ref[...].astype(F32).reshape(1, FF)
    small_ref[2:3, 0:PART] = b2_ref[...].astype(F32).reshape(1, PART)
    diagonal = iota((IMG, IMG), 0) == iota((IMG, IMG), 1)
    caption_row = caption_ref[...]
    caption_high = jnp.right_shift(caption_row, 5)
    caption_low = jnp.bitwise_and(caption_row, 31)

    def as_column(row):
        return jnp.sum(jnp.where(diagonal, row.astype(F32), 0.0), axis=1, keepdims=True)

    text_own_f = jnp.concatenate([text_ref[...].astype(F32), jnp.zeros((IMG, 256 - PART), F32)], axis=1)
    tbuf[a] = text_own_f.astype(BF16)

    def send_text(i, k):
        peer = lax.rem(a + i, GROUP) * GROUP + b
        to_dp(peer, tbuf.at[a], tbuf.at[a], t_send.at[0], t_recv.at[0]).start()
        return k


    for c in range(CH):
        expect(c, 2)
        hand_on(c, across, ahead, 3)
        hand_on(c, across, behind, 4)
        if c == 0:
            expect(c, 0)
            hand_on(c, behind, ahead, 5)
        else:
            expect(c, 1)
            hand_on(c, ahead, behind, 5)

    lax.fori_loop(1, GROUP, send_text, 0)

    targets = target_ref[...]
    named = iota((DP, ROWS), 0) == targets
    named_b = jnp.where(named, 1.0, 0.0).astype(BF16)
    earlier = jnp.where(iota((ROWS, ROWS), 0) < iota((ROWS, ROWS), 1), 1.0, 0.0).astype(BF16)
    before = nn(named_b, earlier)
    rank = jnp.sum(jnp.where(named, before, 0.0), axis=0, keepdims=True).astype(I32)
    code = targets * 16 + rank

    first_row = jnp.where(iota((16, 128), 0) == 0, 1.0, 0.0).astype(BF16)
    b1_row = jnp.broadcast_to(small_ref[0:1, :], (16, FFP))
    b1_b[...] = tn(b1_row.astype(BF16), first_row)
    b2_row = jnp.broadcast_to(small_ref[2:3, 0:256], (16, 256)).astype(BF16)
    b2_b[...] = tn(b2_row, first_row)[0:PART]
    hid[...] = jnp.zeros_like(hid)
    for c in range(CH):
        expect(c, 5)
        hand_on(c, far, across, 6)

    def build_pick(b, k):
        row = iota((128, 1), 0) + b * 128
        slot = jnp.bitwise_and(row, 15)
        base = row - slot
        is_head = slot < CAP
        is_tail = jnp.logical_and(slot >= CAP, slot < CAP + CAP // 2)
        even = base + 2 * (slot - CAP)
        lines = pl.ds(pl.multiple_of(b * 128, 128), 128)
        lane = iota((128, 128), 1)
        main = jnp.where(jnp.where(is_head, row, jnp.where(is_tail, even, -1)) == code, 1.0, 0.0)
        odd = jnp.where(jnp.where(is_tail, even + 1, -1) == code, 1.0, 0.0)
        pick[0, lines, :] = main.astype(BF16)
        pick[1, lines, :] = odd.astype(BF16)
        lack = 1.0 - jnp.sum(main, axis=1, keepdims=True)
        lack_odd = 1.0 - jnp.sum(odd, axis=1, keepdims=True)
        lacks = jnp.where(
            lane == 0,
            jnp.where(is_head, lack, 0.0),
            jnp.where(lane == 1, jnp.where(is_tail, lack, 0.0), jnp.where(lane == 2, jnp.where(is_tail, lack_odd, 0.0), 0.0)),
        )
        empty_pick[lines, :] = lacks.astype(BF16)
        column = iota((128, SLOTS), 1)
        first = jnp.right_shift(row, 4) * CAP
        even_at = first + 2 * (slot - CAP)
        main_at = jnp.where(is_head, first + slot, jnp.where(is_tail, even_at, -1))
        odd_at = jnp.where(is_tail, even_at + 1, -1)
        sel[0, lines, :] = jnp.where(main_at == column, 1.0, 0.0).astype(BF16)
        sel[1, lines, :] = jnp.where(odd_at == column, 1.0, 0.0).astype(BF16)
        return k

    lax.fori_loop(0, DP * 16 // 128, build_pick, 0)

    loads[8].wait()
    loads[9].wait()
    w2t[:, 0:512] = jnp.transpose(w2[0:512, :])
    tail_rows = jnp.concatenate([w2[512:FF, :].astype(F32), jnp.zeros((FFP - FF, FULL), F32)], axis=0)
    w2t[:, 512:FFP] = jnp.transpose(tail_rows).astype(BF16)

    def share(c, member):
        lines = pl.ds(pl.multiple_of(member * PART, 16), PART)
        return nn(w2t[lines, :], hid[:, c * L : (c + 1) * L])

    def pass_on(c, value, member, kind):
        part_out[c, kind] = value.astype(BF16)
        to_member(member, part_out.at[c, kind], part_in.at[c, kind], p_send.at[c], p_recv.at[c, kind]).start()

    def arrived_sum(c, kind):
        to_member(across, part_in.at[c, kind], part_in.at[c, kind], p_send.at[c], p_recv.at[c, kind]).wait_recv()
        return part_in[c, kind].astype(F32)

    def first_sums(c):
        pass_on(c, share(c, far_across), across, 0)
        pass_on(c, share(c, ahead_across), ahead, 1)
        pass_on(c, share(c, behind_across), behind, 2)
        if c == 0:
            pass_on(c, share(c, behind), behind, 5)
        else:
            pass_on(c, share(c, ahead), ahead, 4)

    def second_sums(c):
        pass_on(c, share(c, far) + arrived_sum(c, 0), ahead if c == 0 else behind, 3)
        pass_on(c, share(c, across) + arrived_sum(c, 1) + arrived_sum(c, 2), across, 6)

    def third_sums(c):
        if c == 0:
            pass_on(c, share(c, ahead) + arrived_sum(c, 3), ahead, 4)
        else:
            pass_on(c, share(c, behind) + arrived_sum(c, 3), behind, 5)

    for c in range(CH):
        for kind in (1 if c == 0 else 0, 3, 4, 6):
            expect(c, kind)
        if c == 0:
            for k in range(MP):
                gain_b[k * PART : (k + 1) * PART, :] = tn(xall[0, k, PART:XROWS], first_row)[0:PART]

        rows = xall[c, :, 0:PART].reshape(FULL, L).astype(F32)
        centre = rows - jnp.sum(rows, axis=0, keepdims=True) * (1.0 / FULL)
        spread = jnp.sum(centre * centre, axis=0, keepdims=True) * (1.0 / FULL)
        normed = (centre * lax.rsqrt(spread + 1e-06) * wide(gain_b[...])).astype(BF16)
        pre = nn(w1[...], normed) + wide(b1_b[0:FF, :])
        hid[0:FF, c * L : (c + 1) * L] = gelu(pre).astype(BF16)

        if c < CH - 1:
            first_sums(c)

    first_sums(CH - 1)
    member_f = jnp.where(iota((IMG, ROWS), 0) == owner_ref[...], 1.0, 0.0)
    member = member_f.astype(BF16)
    sums = nt(member, hid[...])
    high = sums.astype(BF16)
    low = (sums - high.astype(F32)).astype(BF16)
    lone = gelu(b1_row).astype(BF16)
    mixed = jnp.concatenate([high, low, lone], axis=0)

    def pool_block(i, k):
        there = lax.rem(m + i, MP)
        lines = pl.ds(pl.multiple_of(there * PART, 16), PART)
        got = nt(mixed, w2t[lines, :])
        pool_out[there, 0:16, 0:PART] = got[0:16] + got[16:32]
        pool_out[there, 16:24, 0:PART] = got[32:40]
        return k

    pool_out[...] = jnp.zeros_like(pool_out)
    lax.fori_loop(0, MP, pool_block, 0)

    def send_pool(i, k):
        there = lax.rem(m + i, MP)
        to_mp(i, pool_out.at[there], pool_in.at[m], pool_send.at[0], pool_recv.at[0]).start()
        return k

    lax.fori_loop(1, MP, send_pool, 0)
    pool_in[m] = pool_out[m]

    for c in range(CH):
        second_sums(c)

    some = pool_in.at[pl.ds(0, MP - 1)]
    to_mp(1, some, some, pool_send.at[0], pool_recv.at[0]).wait_recv()
    pooled = pool_in[0]
    for k in range(1, MP):
        pooled = pooled + pool_in[k]
    b2_wide = jnp.where(iota((1, 256), 1) < PART, small_ref[2:3, 0:256], 0.0)
    counts = jnp.sum(member_f, axis=1, keepdims=True)
    own_sum = nt(member, x_ref[...])
    own_sum = jnp.concatenate([own_sum, jnp.zeros((IMG, 256 - PART), F32)], axis=1)
    image_own = (pooled[0:16] + own_sum) / counts + b2_wide
    empty = (pooled[16:17] + b2_wide).astype(BF16)
    lane = iota((IMG, 256), 1)
    image_note = jnp.where(lane == PART, as_column(caption_high), jnp.where(lane == PART + 1, as_column(caption_low), image_own))
    ibuf[b] = image_note.astype(BF16)

    def send_image(i, k):
        peer = a * GROUP + lax.rem(b + i, GROUP)
        to_dp(peer, ibuf.at[b], ibuf.at[b], i_send.at[0], i_recv.at[0]).start()
        return k

    lax.fori_loop(1, GROUP, send_image, 0)

    for c in range(CH):
        third_sums(c)

    some = tbuf.at[pl.ds(0, GROUP - 1)]
    to_dp(neighbour, some, some, t_send.at[0], t_recv.at[0]).wait_recv()
    some = ibuf.at[pl.ds(0, GROUP - 1)]
    to_dp(neighbour, some, some, i_send.at[0], i_recv.at[0]).wait_recv()
    dots = nt(ibuf[...].reshape(SIDE, 256), tbuf[...].reshape(SIDE, 256))
    feature = iota((1, 256), 1) < PART
    image_f = jnp.where(feature, ibuf[...].reshape(SIDE, 256).astype(F32), 0.0)
    image_sq = jnp.sum(image_f * image_f, axis=1, keepdims=True)
    image_sq = jnp.where(iota((SIDE, SIDE), 1) == 0, image_sq, 0.0)
    text_f = tbuf[...].reshape(SIDE, 256).astype(F32)
    text_f = text_f * text_f
    top = text_f.astype(BF16)
    rest = (text_f - top.astype(F32)).astype(BF16)
    ones = jnp.ones((16, 256), BF16)
    text_sq = (nt(ones, top) + nt(ones, rest))[0:8]
    for k in range(MP):
        pair_out[k, 0:16] = dots[k * IMG : (k + 1) * IMG]
        pair_out[k, 16:32] = image_sq[k * IMG : (k + 1) * IMG]
        pair_out[k, 32:40] = text_sq

    def send_pair(i, k):
        there = lax.rem(m + i, MP)
        to_mp(i, pair_out.at[there], pair_in.at[m], pair_send.at[0], pair_recv.at[0]).start()
        return k

    lax.fori_loop(1, MP, send_pair, 0)
    pair_in[m] = pair_out[m]


    encoded = []
    for c in range(CH):
        total = share(c, m) + arrived_sum(c, 4) + arrived_sum(c, 5) + arrived_sum(c, 6)
        own = x_ref[:, c * L : (c + 1) * L].astype(F32)
        encoded.append(own + total + wide(b2_b[...]))
    encoded = jnp.concatenate(encoded, axis=1)
    by_row = jnp.transpose(jnp.concatenate([encoded, jnp.zeros((256 - PART, ROWS), F32)], axis=0))
    rows_out[:, 0:256] = by_row.astype(BF16)
    rows_out[:, 256:384] = pltpu.roll(by_row[:, 128:256], 16, 1).astype(BF16)
    empty_f = jnp.broadcast_to(empty.astype(F32), (128, 256))
    line = iota((128, 128), 0)
    empty_tail = empty_f[:, 128:256]
    empties = jnp.where(
        line == 0,
        empty_f[:, 0:128],
        jnp.where(line == 1, empty_tail, jnp.where(line == 2, pltpu.roll(empty_tail, 16, 1), 0.0)),
    ).astype(BF16)
    head_row = jnp.bitwise_and(iota((256, 1), 0), 15) < CAP

    def fill(i, k):
        b = lax.rem(s // 16 + 1 + i, DP // 16)
        lines = pl.ds(pl.multiple_of(b * 256, 256), 256)
        main = nn(pick[0, lines, :], rows_out[:, 0:256])
        odd = nn(pick[1, lines, :], rows_out[:, 256:384])
        got = jnp.where(head_row, main[:, 0:128], main[:, 128:256] + odd) + nn(empty_pick[lines, :], empties)
        slot_out[pl.ds(b * 16, 16)] = got.astype(BF16).reshape(16, 16, 128)

        def send_slots(j, k):
            peer = b * 16 + j

            @pl.when(peer != s)
            def _():
                to_dp(peer, slot_out.at[peer], slot_in.at[s], slot_send.at[0], slot_recv.at[0]).start()

            return k

        lax.fori_loop(0, 16, send_slots, 0)
        return k

    lax.fori_loop(0, DP // 16, fill, 0)
    slot_in[s] = slot_out[s]

    some = pair_in.at[pl.ds(0, MP - 1)]
    to_mp(1, some, some, pair_send.at[0], pair_recv.at[0]).wait_recv()
    total = pair_in[0]
    for k in range(1, MP):
        total = total + pair_in[k]
    image_scale = lax.rsqrt(total[16:32, 0:1] + 1e-06)
    text_scale = lax.rsqrt(total[32:33] + 1e-06)
    place = iota((1, SIDE), 1)
    text_name = (jnp.right_shift(place, 4) * (GROUP * IMG) + b * IMG + jnp.bitwise_and(place, 15)).astype(F32)
    noted = ibuf[m].astype(F32)
    caption = noted[:, PART : PART + 1] * 32.0 + noted[:, PART + 1 : PART + 2]
    logits = LOGIT_SCALE * (total[0:16] * image_scale * text_scale) + LOGIT_BIAS
    coef = 1.0 / (1.0 + jnp.exp(-logits)) - jnp.where(caption == text_name, 1.0, 0.0)
    coef_in[m] = jnp.concatenate([coef * text_scale, coef * image_scale], axis=0).astype(BF16)

    def send_coef(i, k):
        to_mp(i, coef_in.at[m], coef_in.at[m], coef_send.at[0], coef_recv.at[0]).start()
        return k

    lax.fori_loop(1, MP, send_coef, 0)
    some = coef_in.at[pl.ds(0, MP - 1)]
    to_mp(1, some, some, coef_send.at[0], coef_recv.at[0]).wait_recv()

    for_images = jnp.concatenate([coef_in[k, 0:16] for k in range(MP)], axis=0)
    for_texts = jnp.concatenate([coef_in[k, 16:32] for k in range(MP)], axis=0)
    part = LOGIT_SCALE * nn(for_images, tbuf[...].reshape(SIDE, 256))
    grad_out[0] = part.astype(BF16).reshape(GROUP, IMG, 256)
    part = LOGIT_SCALE * tn(for_texts, ibuf[...].reshape(SIDE, 256))
    grad_out[1] = part.astype(BF16).reshape(GROUP, IMG, 256)

    def send_grad(i, k):
        there = lax.rem(b + i, GROUP)
        to_dp(a * GROUP + there, grad_out.at[0, there], grad_in.at[0, b], grad_send.at[0], grad_recv.at[0]).start()
        there = lax.rem(a + i, GROUP)
        to_dp(there * GROUP + b, grad_out.at[1, there], grad_in.at[1, a], grad_send.at[1], grad_recv.at[1]).start()
        return k

    lax.fori_loop(1, GROUP, send_grad, 0)
    grad_in[0, b] = grad_out[0, b]
    grad_in[1, a] = grad_out[1, a]

    some = slot_in.at[pl.ds(0, DP - 1)]
    to_dp(neighbour, some, some, slot_send.at[0], slot_recv.at[0]).wait_recv()
    arrived = jnp.transpose(slot_in[...].reshape(DP * 16, 128))
    head_lane = jnp.bitwise_and(iota((1, DP * 16), 1), 15) < CAP
    nothing = jnp.zeros((16, DP * 16), BF16)
    main = jnp.concatenate([jnp.where(head_lane, arrived, 0), jnp.where(head_lane, nothing, arrived[0:16])], axis=0)
    odd = jnp.where(head_lane, nothing, arrived[16:32])
    placed = nn(main, sel[0])
    packed_ref[0:128, :] = placed[0:128].astype(BF16)
    packed_ref[128:PART, :] = (placed[128:PART] + nn(odd, sel[1])).astype(BF16)

    for n, result in enumerate((image_grad_ref, text_grad_ref)):
        some = grad_in.at[n, pl.ds(0, GROUP - 1)]
        to_dp(neighbour, some, some, grad_send.at[n], grad_recv.at[n]).wait_recv()
        sums = grad_in[n, 0].astype(F32)
        for k in range(1, GROUP):
            sums = sums + grad_in[n, k].astype(F32)
        result[...] = sums[:, 0:PART]

    for c in range(CH):
        some = xall.at[c, pl.ds(0, MP - 1), pl.ds(0, XROWS if c == 0 else PART)]
        to_mp(1, some, some, x_send.at[c], x_recv.at[c, 0]).wait_send()
        some = part_out.at[c, pl.ds(0, MP - 1)]
        to_mp(1, some, some, p_send.at[c], p_recv.at[c, 0]).wait_send()
    some = pool_out.at[pl.ds(0, MP - 1)]
    to_mp(1, some, some, pool_send.at[0], pool_recv.at[0]).wait_send()
    some = pair_out.at[pl.ds(0, MP - 1)]
    to_mp(1, some, some, pair_send.at[0], pair_recv.at[0]).wait_send()
    some = coef_in.at[pl.ds(0, MP - 1)]
    to_mp(1, some, some, coef_send.at[0], coef_recv.at[0]).wait_send()
    for buf, send, recv in (
        (tbuf, t_send.at[0], t_recv.at[0]),
        (ibuf, i_send.at[0], i_recv.at[0]),
        (grad_out.at[0], grad_send.at[0], grad_recv.at[0]),
        (grad_out.at[1], grad_send.at[1], grad_recv.at[1]),
    ):
        some = buf.at[pl.ds(0, GROUP - 1)]
        to_dp(neighbour, some, some, send, recv).wait_send()
    some = slot_out.at[pl.ds(0, DP - 1)]
    to_dp(neighbour, some, some, slot_send.at[0], slot_recv.at[0]).wait_send()


def hand_over(packed_in, image_in, text_in, packed_out, image_out, text_out):
    packed_out[...] = packed_in[...]
    image_out[...] = image_in[...]
    text_out[...] = text_in[...]


def shards(patches, patch_shard, patch_image, caption_of, text_embed, ln_gain, fc1_weight, fc1_bias, fc2_weight, fc2_bias):
    vmem = pl.BlockSpec(memory_space=pltpu.VMEM)
    hbm = pl.BlockSpec(memory_space=pltpu.HBM)
    dma = pltpu.SemaphoreType.DMA
    shapes = (
        jax.ShapeDtypeStruct((PART, SLOTS), BF16),
        jax.ShapeDtypeStruct((IMG, PART), F32),
        jax.ShapeDtypeStruct((IMG, PART), F32),
    )
    results = pl.pallas_call(
        kernel,
        out_shape=shapes,
        in_specs=[hbm] * 10,
        out_specs=(vmem, vmem, vmem),
        scratch_shapes=[
            pltpu.VMEM((PART, ROWS), BF16),
            pltpu.VMEM((IMG, PART), BF16),
            pltpu.VMEM((1, ROWS), I32),
            pltpu.VMEM((1, ROWS), I32),
            pltpu.VMEM((1, IMG), I32),
            pltpu.VMEM((PART,), BF16),
            pltpu.VMEM((FF,), BF16),
            pltpu.VMEM((PART,), BF16),
            pltpu.VMEM((FF, FULL), BF16),
            pltpu.VMEM((FF, FULL), BF16),
            pltpu.VMEM((8, FFP), F32),
            pltpu.VMEM((FULL, FFP), BF16),
            pltpu.VMEM((CH, MP, XROWS, L), BF16),
            pltpu.VMEM((FULL, 128), F32),
            pltpu.VMEM((FFP, 128), F32),
            pltpu.VMEM((PART, 128), F32),
            pltpu.VMEM((FFP, ROWS), BF16),
            pltpu.VMEM((CH, 7, PART, L), BF16),
            pltpu.VMEM((CH, 7, PART, L), BF16),
            pltpu.VMEM((MP, 24, 256), F32),
            pltpu.VMEM((MP, 24, 256), F32),
            pltpu.VMEM((GROUP, IMG, 256), BF16),
            pltpu.VMEM((GROUP, IMG, 256), BF16),
            pltpu.VMEM((MP, 40, SIDE), F32),
            pltpu.VMEM((MP, 40, SIDE), F32),
            pltpu.VMEM((MP, 32, SIDE), BF16),
            pltpu.VMEM((2, GROUP, IMG, 256), BF16),
            pltpu.VMEM((2, GROUP, IMG, 256), BF16),
            pltpu.VMEM((2, DP * 16, ROWS), BF16),
            pltpu.VMEM((DP * 16, 128), BF16),
            pltpu.VMEM((2, DP * 16, SLOTS), BF16),
            pltpu.VMEM((ROWS, 384), BF16),
            pltpu.VMEM((DP, 16, 128), BF16),
            pltpu.VMEM((DP, 16, 128), BF16),
            dma((10,)),
            dma((CH,)), dma((CH, 7)),
            dma((1,)), dma((1,)),
            dma((CH,)), dma((CH, 7)),
            dma((1,)), dma((1,)),
            dma((1,)), dma((1,)),
            dma((1,)), dma((1,)),
            dma((1,)), dma((1,)),
            dma((2,)), dma((2,)),
            dma((1,)), dma((1,)),
        ],
        compiler_params=pltpu.CompilerParams(
            collective_id=0, has_side_effects=True, vmem_limit_bytes=60 * 1024 * 1024
        ),
    )(
        patches.T, text_embed, patch_shard.reshape(1, ROWS), patch_image, caption_of.reshape(1, IMG),
        ln_gain, fc1_bias, fc2_bias, fc1_weight.T, fc2_weight,
    )
    packed, image_grad, text_grad = pl.pallas_call(
        hand_over,
        out_shape=shapes,
        in_specs=[vmem] * 3,
        out_specs=(vmem,) * 3,
        compiler_params=pltpu.CompilerParams(vmem_limit_bytes=60 * 1024 * 1024),
    )(*results)
    return packed.T[None], image_grad, text_grad


def solution(mesh):
    return jax.shard_map(
        shards,
        mesh=mesh,
        in_specs=(
            P("dp", "mp"),
            P("dp", None),
            P("dp", None),
            P("dp"),
            P("dp", "mp"),
            P("mp"),
            P(None, "mp"),
            P("mp"),
            P("mp", None),
            P("mp"),
        ),
        out_specs=(P("dp", None, "mp"), P("dp", "mp"), P("dp", "mp")),
        check_vma=False,
    )
```

time: 988 us -> 71 us (0.07)
  waiting for transfers between devices: 540 us -> 0 us
  starting transfers between devices: 273 us -> 0 us
  blocking collectives: 86.6 us -> 0 us
  Pallas kernels: 0 us -> 70.2 us
  matrix products: 36.2 us -> 0 us
  local copies, waits for them, and re-layouts: 16 us -> 0 us
  between operations: 14.7 us -> 0.64 us
    ppermute x128 -> x0, waiting for transfers between devices: 404 us -> none  [shifted(): return lax.ppermute(value, axis, pairs)]
    ppermute x128 -> x0, starting transfers between devices: 254 us -> none  [shifted(): return lax.ppermute(value, axis, pairs)]
    pallas_call x0 -> x2, Pallas kernels: none -> 70.2 us  [the longest x1 68.6 us: shards(): pl.pallas_call(kernel, out_shape=shapes, in_specs=[hbm] * 10, out_specs=(...]
    reduce_scatter x1 -> x0, waiting for transfers between devices: 68.5 us -> none  [encode_block(): lax.psum_scatter(partial_out, 'mp', scatter_dimension=1, tiled=True)]
    all_to_all x2 -> x0, blocking collectives: 48 us -> none  [the longest x1 40.6 us: shards(): lax.all_to_all(outgoing, 'dp', split_axis=0, concat_axis=0, tiled=True)]
    dot_general x194 -> x0, matrix products: 36.2 us -> none  [the longest x64 13 us: score(): jnp.dot(pair_coef, text_block, preferred_element_type=jnp.float32)]
    all_to_all x2 -> x0, waiting for transfers between devices: 25.4 us -> none  [the longest x1 20.6 us: shards(): lax.all_to_all(coded, 'dp', split_axis=0, concat_axis=0, tiled=True)]
    unnamed x4 -> x0, waiting for transfers between devices: 24 us -> none
  transfers between devices with their start and end apart: 133 -> 0, of which waited for: 132 -> 0; matrix products, arithmetic and copies ran while one was open for 3% -> 0% of each run, Pallas kernels for 0% -> 0%
where the time goes in v1:
time: 71 us; the launch traced here: 70.8 us
  Pallas kernels  70.2 us (99%)
    pallas_call x1, Pallas kernels, shards(): pl.pallas_call(kernel, out_shape=shapes, in_specs=[hbm] * 10, out_specs=(...  68.6 us
    pallas_call x1, Pallas kernels, shards(): pl.pallas_call(hand_over, out_shape=shapes, in_specs=[vmem] * 3, out_spec...  1.63 us

profile of v1, /device:TPU:1, one launch (start us, length us, event | category | flops | bytes accessed | tf_op | source)
XLA Modules:
  0.0 70.8 jit_solution(2469713411490018637)
XLA Ops:
  0.6 68.6 %shard_map.121 = (bf16[144,640]{1,0:T(8,128)(2,1)}, f32[16,144]{1,0:T(8,128)}, f32[16,144]{1,0:T(8,128)}) custom-call(bf16[144,512]{1,0:T(8,128)(2,1)} %bitcast.8, bf16[16,144]{1,0:T(8,128)(2,1)} %text_hbm.1, s32[1,512]{1,0:T(1,128)} %bitcast.9, s32[1,512]{1,0:T(1,128)} %owner_hbm.1, s32[1,16]{1,0:T(1,128)} %bitcast.10, bf16[144]{0:T(256)(128)(2,1)} %gain_hbm.1, ...), custom_call_target="tpu_custom_call" | custom-call | tf_op jit(solution)/shard_map/pallas_call | solution.py:507
  69.2 1.6 %shard_map.122 = (bf16[144,640]{1,0:T(8,128)(2,1)}, f32[16,144]{1,0:T(8,128)}, f32[16,144]{1,0:T(8,128)}) custom-call(bf16[144,640]{1,0:T(8,128)(2,1)} %get-tuple-element.9.packed_in, f32[16,144]{1,0:T(8,128)} %get-tuple-element.10.image_in, f32[16,144]{1,0:T(8,128)} %get-tuple-element.11.text_in), custom_call_target="tpu_custom_call" | custom-call | tf_op jit(solution)/shard_map/pallas_call | solution.py:565

commit v2 on v1

--- a/solution.py
+++ b/solution.py
@@ -96,11 +96,14 @@
         return c
 
     def greet_dp(i, c):
-        pl.semaphore_signal(barrier, inc=1, device_id=(lax.rem(s + i, DP), m), device_id_type=MESH)
+        images = a * GROUP + lax.rem(b + i, GROUP)
+        texts = lax.rem(a + i, GROUP) * GROUP + b
+        pl.semaphore_signal(barrier, inc=1, device_id=(images, m), device_id_type=MESH)
+        pl.semaphore_signal(barrier, inc=1, device_id=(texts, m), device_id_type=MESH)
         return c
 
-    lax.fori_loop(1, MP, greet_mp, 0)
-    lax.fori_loop(1, DP, greet_dp, 0)
+    lax.fori_loop(1, MP, greet_mp, 0, unroll=True)
+    lax.fori_loop(1, GROUP, greet_dp, 0, unroll=True)
 
     def to_member(member, src, dst, send, recv):
         return pltpu.make_async_remote_copy(
@@ -125,7 +128,7 @@
         xall[c, m, 0:PART] = x_ref[:, c * L : (c + 1) * L]
     xall[0, m, PART:XROWS] = jnp.broadcast_to(small_ref[1:2, 0:L], (XROWS - PART, L)).astype(BF16)
 
-    pl.semaphore_wait(barrier, DP + MP - 2)
+    pl.semaphore_wait(barrier, MP - 1 + 2 * (GROUP - 1))
 
     def block(c, member):
         return xall.at[c, member, pl.ds(0, XROWS if c == 0 else PART)]
@@ -163,17 +166,17 @@
 
 
     for c in range(CH):
-        expect(c, 2)
-        hand_on(c, across, ahead, 3)
-        hand_on(c, across, behind, 4)
         if c == 0:
             expect(c, 0)
             hand_on(c, behind, ahead, 5)
         else:
             expect(c, 1)
             hand_on(c, ahead, behind, 5)
-
-    lax.fori_loop(1, GROUP, send_text, 0)
+        expect(c, 2)
+        hand_on(c, across, ahead, 3)
+        hand_on(c, across, behind, 4)
+
+    lax.fori_loop(1, GROUP, send_text, 0, unroll=True)
 
     targets = target_ref[...]
     named = iota((DP, ROWS), 0) == targets
@@ -304,7 +307,7 @@
         to_mp(i, pool_out.at[there], pool_in.at[m], pool_send.at[0], pool_recv.at[0]).start()
         return k
 
-    lax.fori_loop(1, MP, send_pool, 0)
+    lax.fori_loop(1, MP, send_pool, 0, unroll=True)
     pool_in[m] = pool_out[m]
 
     for c in range(CH):
@@ -325,18 +328,19 @@
     image_note = jnp.where(lane == PART, as_column(caption_high), jnp.where(lane == PART + 1, as_column(caption_low), image_own))
     ibuf[b] = image_note.astype(BF16)
 
+    some = tbuf.at[pl.ds(0, GROUP - 1)]
+    to_dp(neighbour, some, some, t_send.at[0], t_recv.at[0]).wait_recv()
+
     def send_image(i, k):
         peer = a * GROUP + lax.rem(b + i, GROUP)
         to_dp(peer, ibuf.at[b], ibuf.at[b], i_send.at[0], i_recv.at[0]).start()
         return k
 
-    lax.fori_loop(1, GROUP, send_image, 0)
+    lax.fori_loop(1, GROUP, send_image, 0, unroll=True)
 
     for c in range(CH):
         third_sums(c)
 
-    some = tbuf.at[pl.ds(0, GROUP - 1)]
-    to_dp(neighbour, some, some, t_send.at[0], t_recv.at[0]).wait_recv()
     some = ibuf.at[pl.ds(0, GROUP - 1)]
     to_dp(neighbour, some, some, i_send.at[0], i_recv.at[0]).wait_recv()
     dots = nt(ibuf[...].reshape(SIDE, 256), tbuf[...].reshape(SIDE, 256))
@@ -360,7 +364,7 @@
         to_mp(i, pair_out.at[there], pair_in.at[m], pair_send.at[0], pair_recv.at[0]).start()
         return k
 
-    lax.fori_loop(1, MP, send_pair, 0)
+    lax.fori_loop(1, MP, send_pair, 0, unroll=True)
     pair_in[m] = pair_out[m]
 
 
@@ -383,27 +387,27 @@
     ).astype(BF16)
     head_row = jnp.bitwise_and(iota((256, 1), 0), 15) < CAP
 
-    def fill(i, k):
-        b = lax.rem(s // 16 + 1 + i, DP // 16)
-        lines = pl.ds(pl.multiple_of(b * 256, 256), 256)
+    def fill(block):
+        lines = pl.ds(pl.multiple_of(block * 256, 256), 256)
         main = nn(pick[0, lines, :], rows_out[:, 0:256])
         odd = nn(pick[1, lines, :], rows_out[:, 256:384])
         got = jnp.where(head_row, main[:, 0:128], main[:, 128:256] + odd) + nn(empty_pick[lines, :], empties)
-        slot_out[pl.ds(b * 16, 16)] = got.astype(BF16).reshape(16, 16, 128)
-
-        def send_slots(j, k):
-            peer = b * 16 + j
-
-            @pl.when(peer != s)
-            def _():
-                to_dp(peer, slot_out.at[peer], slot_in.at[s], slot_send.at[0], slot_recv.at[0]).start()
-
-            return k
-
-        lax.fori_loop(0, 16, send_slots, 0)
-        return k
-
-    lax.fori_loop(0, DP // 16, fill, 0)
+        slot_out[pl.ds(block * 16, 16)] = got.astype(BF16).reshape(16, 16, 128)
+
+    def send_slot(peer):
+        to_dp(peer, slot_out.at[peer], slot_in.at[s], slot_send.at[0], slot_recv.at[0]).start()
+
+    def fill_other(i, k):
+        block = lax.rem(s // 16 + i, DP // 16)
+        fill(block)
+        for j in range(16):
+            send_slot(block * 16 + j)
+        return k
+
+    lax.fori_loop(1, DP // 16, fill_other, 0)
+    fill(s // 16)
+    for j in range(1, 16):
+        send_slot(s // 16 * 16 + lax.rem(s + j, 16))
     slot_in[s] = slot_out[s]
 
     some = pair_in.at[pl.ds(0, MP - 1)]
@@ -425,7 +429,7 @@
         to_mp(i, coef_in.at[m], coef_in.at[m], coef_send.at[0], coef_recv.at[0]).start()
         return k
 
-    lax.fori_loop(1, MP, send_coef, 0)
+    lax.fori_loop(1, MP, send_coef, 0, unroll=True)
     some = coef_in.at[pl.ds(0, MP - 1)]
     to_mp(1, some, some, coef_send.at[0], coef_recv.at[0]).wait_recv()
 
@@ -443,7 +447,7 @@
         to_dp(there * GROUP + b, grad_out.at[1, there], grad_in.at[1, a], grad_send.at[1], grad_recv.at[1]).start()
         return k
 
-    lax.fori_loop(1, GROUP, send_grad, 0)
+    lax.fori_loop(1, GROUP, send_grad, 0, unroll=True)
     grad_in[0, b] = grad_out[0, b]
     grad_in[1, a] = grad_out[1, a]
 

time: 71 us -> 67.8 us (0.955)
  Pallas kernels: 70.2 us -> 67 us
    pallas_call x1, Pallas kernels: 68.6 us -> 65.4 us  [shards(): pl.pallas_call(kernel, out_shape=shapes, in_specs=[hbm] * 10, out_specs=(...]
where the time goes in v2:
time: 67.8 us; the launch traced here: 67.7 us
  Pallas kernels  67 us (99%)
    pallas_call x1, Pallas kernels, shards(): pl.pallas_call(kernel, out_shape=shapes, in_specs=[hbm] * 10, out_specs=(...  65.4 us
    pallas_call x1, Pallas kernels, shards(): pl.pallas_call(hand_over, out_shape=shapes, in_specs=[vmem] * 3, out_spec...  1.63 us

profile of v2, /device:TPU:1, one launch (start us, length us, event | category | flops | bytes accessed | tf_op | source)
XLA Modules:
  0.0 67.7 jit_solution(16225334097400815392)
XLA Ops:
  0.6 65.4 %shard_map.121 = (bf16[144,640]{1,0:T(8,128)(2,1)}, f32[16,144]{1,0:T(8,128)}, f32[16,144]{1,0:T(8,128)}) custom-call(bf16[144,512]{1,0:T(8,128)(2,1)} %bitcast.8, bf16[16,144]{1,0:T(8,128)(2,1)} %text_hbm.1, s32[1,512]{1,0:T(1,128)} %bitcast.9, s32[1,512]{1,0:T(1,128)} %owner_hbm.1, s32[1,16]{1,0:T(1,128)} %bitcast.10, bf16[144]{0:T(256)(128)(2,1)} %gain_hbm.1, ...), custom_call_target="tpu_custom_call" | custom-call | tf_op jit(solution)/shard_map/pallas_call | solution.py:511
  66.0 1.6 %shard_map.122 = (bf16[144,640]{1,0:T(8,128)(2,1)}, f32[16,144]{1,0:T(8,128)}, f32[16,144]{1,0:T(8,128)}) custom-call(bf16[144,640]{1,0:T(8,128)(2,1)} %get-tuple-element.9.packed_in, f32[16,144]{1,0:T(8,128)} %get-tuple-element.10.image_in, f32[16,144]{1,0:T(8,128)} %get-tuple-element.11.text_in), custom_call_target="tpu_custom_call" | custom-call | tf_op jit(solution)/shard_map/pallas_call | solution.py:569

commit v3 on v2

--- a/solution.py
+++ b/solution.py
@@ -54,9 +54,9 @@
     x_hbm, text_hbm, target_hbm, owner_hbm, caption_hbm, gain_hbm, b1_hbm, b2_hbm, w1_hbm, w2_hbm,
     packed_ref, image_grad_ref, text_grad_ref,
     x_ref, text_ref, target_ref, owner_ref, caption_ref, gain_ref, b1_ref, b2_ref, w1, w2,
-    small_ref, w2t, xall, gain_b, b1_b, b2_b, hid, part_out, part_in,
+    small_ref, w2t, xall, gain_b, b1_b, b2_b, normed, hid, shares, part_out, part_in,
     pool_out, pool_in, tbuf, ibuf, pair_out, pair_in, coef_in, grad_out, grad_in,
-    pick, empty_pick, sel, rows_out, slot_out, slot_in,
+    earlier, pick, empty_pick, sel, rows_out, slot_out, slot_in,
     load_sem, x_send, x_recv, t_send, t_recv, p_send, p_recv,
     pool_send, pool_recv, i_send, i_recv, pair_send, pair_recv, coef_send, coef_recv,
     grad_send, grad_recv, slot_send, slot_recv,
@@ -126,12 +126,12 @@
     small_ref[1:2, 0:PART] = gain_ref[...].astype(F32).reshape(1, PART)
     for c in range(CH):
         xall[c, m, 0:PART] = x_ref[:, c * L : (c + 1) * L]
-    xall[0, m, PART:XROWS] = jnp.broadcast_to(small_ref[1:2, 0:L], (XROWS - PART, L)).astype(BF16)
+        xall[c, m, PART:XROWS] = jnp.broadcast_to(small_ref[1:2, 0:L], (XROWS - PART, L)).astype(BF16)
 
     pl.semaphore_wait(barrier, MP - 1 + 2 * (GROUP - 1))
 
     def block(c, member):
-        return xall.at[c, member, pl.ds(0, XROWS if c == 0 else PART)]
+        return xall.at[c, member]
 
     def hand_on(c, owner, member, kind):
         to_member(member, block(c, owner), block(c, owner), x_send.at[c], x_recv.at[c, kind]).start()
@@ -139,10 +139,13 @@
     def expect(c, kind):
         to_member(across, block(c, m), block(c, m), x_send.at[c], x_recv.at[c, kind]).wait_recv()
 
-    for c in range(CH):
+    def hand_own(c, k):
         hand_on(c, m, across, 2)
         hand_on(c, m, ahead, 0)
         hand_on(c, m, behind, 1)
+        return k
+
+    lax.fori_loop(0, CH, hand_own, 0)
 
     for load in loads[2:8]:
         load.wait()
@@ -165,26 +168,41 @@
         return k
 
 
-    for c in range(CH):
-        if c == 0:
-            expect(c, 0)
-            hand_on(c, behind, ahead, 5)
-        else:
-            expect(c, 1)
-            hand_on(c, ahead, behind, 5)
+    def onward(c):
+        return lax.rem(ring + 1 + 2 * c, 4) * 2 + side
+
+    def backward(c):
+        return lax.rem(ring + 3 + 2 * c, 4) * 2 + side
+
+    def hand_first(c, k):
+        expect(c, c)
+        hand_on(c, backward(c), onward(c), 5)
         expect(c, 2)
         hand_on(c, across, ahead, 3)
         hand_on(c, across, behind, 4)
+        return k
+
+    def hand_last(c, k):
+        expect(c, 5)
+        hand_on(c, far, across, 6)
+        return k
 
     lax.fori_loop(1, GROUP, send_text, 0, unroll=True)
 
-    targets = target_ref[...]
-    named = iota((DP, ROWS), 0) == targets
-    named_b = jnp.where(named, 1.0, 0.0).astype(BF16)
-    earlier = jnp.where(iota((ROWS, ROWS), 0) < iota((ROWS, ROWS), 1), 1.0, 0.0).astype(BF16)
-    before = nn(named_b, earlier)
-    rank = jnp.sum(jnp.where(named, before, 0.0), axis=0, keepdims=True).astype(I32)
-    code = targets * 16 + rank
+    lax.fori_loop(0, CH, hand_first, 0)
+
+    loads[8].wait()
+    loads[9].wait()
+
+    def turn(n, k):
+        lines = pl.ds(pl.multiple_of(n * 128, 128), 128)
+        w2t[lines, 0:512] = jnp.transpose(w2[0:512, lines])
+        last = jnp.concatenate([w2[512:FF, lines].astype(F32), jnp.zeros((FFP - FF, 128), F32)], axis=0)
+        w2t[lines, 512:FFP] = jnp.transpose(last).astype(BF16)
+        return k
+
+    lax.fori_loop(0, FULL // 128, turn, 0)
+    lax.fori_loop(0, CH, hand_last, 0)
 
     first_row = jnp.where(iota((16, 128), 0) == 0, 1.0, 0.0).astype(BF16)
     b1_row = jnp.broadcast_to(small_ref[0:1, :], (16, FFP))
@@ -192,9 +210,145 @@
     b2_row = jnp.broadcast_to(small_ref[2:3, 0:256], (16, 256)).astype(BF16)
     b2_b[...] = tn(b2_row, first_row)[0:PART]
     hid[...] = jnp.zeros_like(hid)
-    for c in range(CH):
-        expect(c, 5)
-        hand_on(c, far, across, 6)
+
+    targets = target_ref[...]
+    named = iota((DP, ROWS), 0) == targets
+    named_b = jnp.where(named, 1.0, 0.0).astype(BF16)
+
+    def build_earlier(n, k):
+        lines = pl.ds(pl.multiple_of(n * 128, 128), 128)
+        earlier[lines, :] = jnp.where(iota((128, ROWS), 0) + n * 128 < iota((128, ROWS), 1), 1.0, 0.0).astype(BF16)
+        return k
+
+    lax.fori_loop(0, ROWS // 128, build_earlier, 0)
+    before = nn(named_b, earlier[...])
+    rank = jnp.sum(jnp.where(named, before, 0.0), axis=0, keepdims=True).astype(I32)
+    code = targets * 16 + rank
+
+    def pass_on(c, value, member, kind):
+        part_out[c, kind] = value.astype(BF16)
+        to_member(member, part_out.at[c, kind], part_in.at[c, kind], p_send.at[c], p_recv.at[c, kind]).start()
+
+    def arrived_sum(c, kind):
+        to_member(across, part_in.at[c, kind], part_in.at[c, kind], p_send.at[c], p_recv.at[c, kind]).wait_recv()
+        return part_in[c, kind].astype(F32)
+
+    def second_sums(c):
+        pass_on(c, shares[c, far] + arrived_sum(c, 0), onward(c), 3)
+        pass_on(c, shares[c, across] + arrived_sum(c, 1) + arrived_sum(c, 2), across, 6)
+
+    def third_sums(c):
+        pass_on(c, shares[c, onward(c)] + arrived_sum(c, 3), onward(c), 4 + c)
+
+    def chunk(c, k):
+        for kind in (1 - c, 3, 4, 6):
+            expect(c, kind)
+
+        @pl.when(c == 0)
+        def _():
+            def gains(n, k):
+                lines = pl.ds(pl.multiple_of(n * PART, 16), PART)
+                gain_b[lines, :] = tn(xall[0, n, PART:XROWS], first_row)[0:PART]
+                return k
+
+            lax.fori_loop(0, MP, gains, 0)
+
+        def rows(n):
+            return xall[c, n, 0:PART].astype(F32)
+
+        def add_rows(n, total):
+            return total + jnp.sum(rows(n), axis=0, keepdims=True)
+
+        mean = lax.fori_loop(0, MP, add_rows, jnp.zeros((1, L), F32)) * (1.0 / FULL)
+
+        def add_squares(n, total):
+            centre = rows(n) - mean
+            return total + jnp.sum(centre * centre, axis=0, keepdims=True)
+
+        spread = lax.fori_loop(0, MP, add_squares, jnp.zeros((1, L), F32)) * (1.0 / FULL)
+        inverse = lax.rsqrt(spread + 1e-06)
+
+        def norm_rows(n, k):
+            lines = pl.ds(pl.multiple_of(n * PART, 16), PART)
+            normed[lines, :] = ((rows(n) - mean) * inverse * wide(gain_b[lines, :])).astype(BF16)
+            return k
+
+        lax.fori_loop(0, MP, norm_rows, 0)
+        pre = nn(w1[...], normed[...]) + wide(b1_b[0:FF, :])
+        hid[c, 0:FF, :] = gelu(pre).astype(BF16)
+
+        def share(n, k):
+            member = lax.rem(ring + 2 + 3 * n, 4) * 2 + lax.rem(side + 1 + n // 4, 2)
+            lines = pl.ds(pl.multiple_of(member * PART, 16), PART)
+            shares[c, member] = nn(w2t[lines, :], hid[c])
+            return k
+
+        lax.fori_loop(0, MP, share, 0)
+        pass_on(c, shares[c, far_across], across, 0)
+        pass_on(c, shares[c, ahead_across], ahead, 1)
+        pass_on(c, shares[c, behind_across], behind, 2)
+        pass_on(c, shares[c, backward(c)], backward(c), 5 - c)
+        return k
+
+    lax.fori_loop(0, CH, chunk, 0)
+    second_sums(0)
+
+    member_f = jnp.where(iota((IMG, ROWS), 0) == owner_ref[...], 1.0, 0.0)
+    member = member_f.astype(BF16)
+    sums = nt(member[:, 0:L], hid[0]) + nt(member[:, L:ROWS], hid[1])
+    high = sums.astype(BF16)
+    low = (sums - high.astype(F32)).astype(BF16)
+    lone = gelu(b1_row).astype(BF16)
+    mixed = jnp.concatenate([high, low, lone], axis=0)
+
+    def pool_block(i, k):
+        there = lax.rem(m + i, MP)
+        lines = pl.ds(pl.multiple_of(there * PART, 16), PART)
+        got = nt(mixed, w2t[lines, :])
+        pool_out[there, 0:16, 0:PART] = got[0:16] + got[16:32]
+        pool_out[there, 16:24, 0:PART] = got[32:40]
+        return k
+
+    pool_out[...] = jnp.zeros_like(pool_out)
+    lax.fori_loop(0, MP, pool_block, 0)
+
+    def send_pool(i, k):
+        there = lax.rem(m + i, MP)
+        to_mp(i, pool_out.at[there], pool_in.at[m], pool_send.at[0], pool_recv.at[0]).start()
+        return k
+
+    lax.fori_loop(1, MP, send_pool, 0, unroll=True)
+    pool_in[m] = pool_out[m]
+
+    second_sums(1)
+    third_sums(0)
+
+    some = pool_in.at[pl.ds(0, MP - 1)]
+    to_mp(1, some, some, pool_send.at[0], pool_recv.at[0]).wait_recv()
+    pooled = pool_in[0]
+    for k in range(1, MP):
+        pooled = pooled + pool_in[k]
+    b2_wide = jnp.where(iota((1, 256), 1) < PART, small_ref[2:3, 0:256], 0.0)
+    counts = jnp.sum(member_f, axis=1, keepdims=True)
+    own_sum = nt(member, x_ref[...])
+    own_sum = jnp.concatenate([own_sum, jnp.zeros((IMG, 256 - PART), F32)], axis=1)
+    image_own = (pooled[0:16] + own_sum) / counts + b2_wide
+    empty = (pooled[16:17] + b2_wide).astype(BF16)
+    lane = iota((IMG, 256), 1)
+    image_note = jnp.where(lane == PART, as_column(caption_high), jnp.where(lane == PART + 1, as_column(caption_low), image_own))
+    ibuf[b] = image_note.astype(BF16)
+
+    some = tbuf.at[pl.ds(0, GROUP - 1)]
+    to_dp(neighbour, some, some, t_send.at[0], t_recv.at[0]).wait_recv()
+
+    def send_image(i, k):
+        peer = a * GROUP + lax.rem(b + i, GROUP)
+        to_dp(peer, ibuf.at[b], ibuf.at[b], i_send.at[0], i_recv.at[0]).start()
+        return k
+
+    lax.fori_loop(1, GROUP, send_image, 0, unroll=True)
+
+    third_sums(1)
 
     def build_pick(b, k):
         row = iota((128, 1), 0) + b * 128
@@ -228,118 +382,6 @@
 
     lax.fori_loop(0, DP * 16 // 128, build_pick, 0)
 
-    loads[8].wait()
-    loads[9].wait()
-    w2t[:, 0:512] = jnp.transpose(w2[0:512, :])
-    tail_rows = jnp.concatenate([w2[512:FF, :].astype(F32), jnp.zeros((FFP - FF, FULL), F32)], axis=0)
-    w2t[:, 512:FFP] = jnp.transpose(tail_rows).astype(BF16)
-
-    def share(c, member):
-        lines = pl.ds(pl.multiple_of(member * PART, 16), PART)
-        return nn(w2t[lines, :], hid[:, c * L : (c + 1) * L])
-
-    def pass_on(c, value, member, kind):
-        part_out[c, kind] = value.astype(BF16)
-        to_member(member, part_out.at[c, kind], part_in.at[c, kind], p_send.at[c], p_recv.at[c, kind]).start()
-
-    def arrived_sum(c, kind):
-        to_member(across, part_in.at[c, kind], part_in.at[c, kind], p_send.at[c], p_recv.at[c, kind]).wait_recv()
-        return part_in[c, kind].astype(F32)
-
-    def first_sums(c):
-        pass_on(c, share(c, far_across), across, 0)
-        pass_on(c, share(c, ahead_across), ahead, 1)
-        pass_on(c, share(c, behind_across), behind, 2)
-        if c == 0:
-            pass_on(c, share(c, behind), behind, 5)
-        else:
-            pass_on(c, share(c, ahead), ahead, 4)
-
-    def second_sums(c):
-        pass_on(c, share(c, far) + arrived_sum(c, 0), ahead if c == 0 else behind, 3)
-        pass_on(c, share(c, across) + arrived_sum(c, 1) + arrived_sum(c, 2), across, 6)
-
-    def third_sums(c):
-        if c == 0:
-            pass_on(c, share(c, ahead) + arrived_sum(c, 3), ahead, 4)
-        else:
-            pass_on(c, share(c, behind) + arrived_sum(c, 3), behind, 5)
-
-    for c in range(CH):
-        for kind in (1 if c == 0 else 0, 3, 4, 6):
-            expect(c, kind)
-        if c == 0:
-            for k in range(MP):
-                gain_b[k * PART : (k + 1) * PART, :] = tn(xall[0, k, PART:XROWS], first_row)[0:PART]
-
-        rows = xall[c, :, 0:PART].reshape(FULL, L).astype(F32)
-        centre = rows - jnp.sum(rows, axis=0, keepdims=True) * (1.0 / FULL)
-        spread = jnp.sum(centre * centre, axis=0, keepdims=True) * (1.0 / FULL)
-        normed = (centre * lax.rsqrt(spread + 1e-06) * wide(gain_b[...])).astype(BF16)
-        pre = nn(w1[...], normed) + wide(b1_b[0:FF, :])
-        hid[0:FF, c * L : (c + 1) * L] = gelu(pre).astype(BF16)
-
-        if c < CH - 1:
-            first_sums(c)
-
-    first_sums(CH - 1)
-    member_f = jnp.where(iota((IMG, ROWS), 0) == owner_ref[...], 1.0, 0.0)
-    member = member_f.astype(BF16)
-    sums = nt(member, hid[...])
-    high = sums.astype(BF16)
-    low = (sums - high.astype(F32)).astype(BF16)
-    lone = gelu(b1_row).astype(BF16)
-    mixed = jnp.concatenate([high, low, lone], axis=0)
-
-    def pool_block(i, k):
-        there = lax.rem(m + i, MP)
-        lines = pl.ds(pl.multiple_of(there * PART, 16), PART)
-        got = nt(mixed, w2t[lines, :])
-        pool_out[there, 0:16, 0:PART] = got[0:16] + got[16:32]
-        pool_out[there, 16:24, 0:PART] = got[32:40]
-        return k
-
-    pool_out[...] = jnp.zeros_like(pool_out)
-    lax.fori_loop(0, MP, pool_block, 0)
-
-    def send_pool(i, k):
-        there = lax.rem(m + i, MP)
-        to_mp(i, pool_out.at[there], pool_in.at[m], pool_send.at[0], pool_recv.at[0]).start()
-        return k
-
-    lax.fori_loop(1, MP, send_pool, 0, unroll=True)
-    pool_in[m] = pool_out[m]
-
-    for c in range(CH):
-        second_sums(c)
-
-    some = pool_in.at[pl.ds(0, MP - 1)]
-    to_mp(1, some, some, pool_send.at[0], pool_recv.at[0]).wait_recv()
-    pooled = pool_in[0]
-    for k in range(1, MP):
-        pooled = pooled + pool_in[k]
-    b2_wide = jnp.where(iota((1, 256), 1) < PART, small_ref[2:3, 0:256], 0.0)
-    counts = jnp.sum(member_f, axis=1, keepdims=True)
-    own_sum = nt(member, x_ref[...])
-    own_sum = jnp.concatenate([own_sum, jnp.zeros((IMG, 256 - PART), F32)], axis=1)
-    image_own = (pooled[0:16] + own_sum) / counts + b2_wide
-    empty = (pooled[16:17] + b2_wide).astype(BF16)
-    lane = iota((IMG, 256), 1)
-    image_note = jnp.where(lane == PART, as_column(caption_high), jnp.where(lane == PART + 1, as_column(caption_low), image_own))
-    ibuf[b] = image_note.astype(BF16)
-
-    some = tbuf.at[pl.ds(0, GROUP - 1)]
-    to_dp(neighbour, some, some, t_send.at[0], t_recv.at[0]).wait_recv()
-
-    def send_image(i, k):
-        peer = a * GROUP + lax.rem(b + i, GROUP)
-        to_dp(peer, ibuf.at[b], ibuf.at[b], i_send.at[0], i_recv.at[0]).start()
-        return k
-
-    lax.fori_loop(1, GROUP, send_image, 0, unroll=True)
-
-    for c in range(CH):
-        third_sums(c)
 
     some = ibuf.at[pl.ds(0, GROUP - 1)]
     to_dp(neighbour, some, some, i_send.at[0], i_recv.at[0]).wait_recv()
@@ -368,15 +410,16 @@
     pair_in[m] = pair_out[m]
 
 
-    encoded = []
-    for c in range(CH):
-        total = share(c, m) + arrived_sum(c, 4) + arrived_sum(c, 5) + arrived_sum(c, 6)
-        own = x_ref[:, c * L : (c + 1) * L].astype(F32)
-        encoded.append(own + total + wide(b2_b[...]))
-    encoded = jnp.concatenate(encoded, axis=1)
-    by_row = jnp.transpose(jnp.concatenate([encoded, jnp.zeros((256 - PART, ROWS), F32)], axis=0))
-    rows_out[:, 0:256] = by_row.astype(BF16)
-    rows_out[:, 256:384] = pltpu.roll(by_row[:, 128:256], 16, 1).astype(BF16)
+    def finish(c, k):
+        total = shares[c, m] + arrived_sum(c, 4) + arrived_sum(c, 5) + arrived_sum(c, 6)
+        encoded = xall[c, m, 0:PART].astype(F32) + total + wide(b2_b[...])
+        by_row = jnp.transpose(jnp.concatenate([encoded, jnp.zeros((256 - PART, L), F32)], axis=0))
+        lines = pl.ds(pl.multiple_of(c * L, 128), L)
+        rows_out[lines, 0:256] = by_row.astype(BF16)
+        rows_out[lines, 256:384] = pltpu.roll(by_row[:, 128:256], 16, 1).astype(BF16)
+        return k
+
+    lax.fori_loop(0, CH, finish, 0)
     empty_f = jnp.broadcast_to(empty.astype(F32), (128, 256))
     line = iota((128, 128), 0)
     empty_tail = empty_f[:, 128:256]
@@ -387,27 +430,23 @@
     ).astype(BF16)
     head_row = jnp.bitwise_and(iota((256, 1), 0), 15) < CAP
 
-    def fill(block):
+    def send_slot(peer):
+        to_dp(peer, slot_out.at[peer], slot_in.at[s], slot_send.at[0], slot_recv.at[0]).start()
+
+    def fill(i, k):
+        block = lax.rem(s // 16 + i, DP // 16)
         lines = pl.ds(pl.multiple_of(block * 256, 256), 256)
         main = nn(pick[0, lines, :], rows_out[:, 0:256])
         odd = nn(pick[1, lines, :], rows_out[:, 256:384])
         got = jnp.where(head_row, main[:, 0:128], main[:, 128:256] + odd) + nn(empty_pick[lines, :], empties)
         slot_out[pl.ds(block * 16, 16)] = got.astype(BF16).reshape(16, 16, 128)
-
-    def send_slot(peer):
-        to_dp(peer, slot_out.at[peer], slot_in.at[s], slot_send.at[0], slot_recv.at[0]).start()
-
-    def fill_other(i, k):
-        block = lax.rem(s // 16 + i, DP // 16)
-        fill(block)
-        for j in range(16):
-            send_slot(block * 16 + j)
-        return k
-
-    lax.fori_loop(1, DP // 16, fill_other, 0)
-    fill(s // 16)
-    for j in range(1, 16):
-        send_slot(s // 16 * 16 + lax.rem(s + j, 16))
+        for j in range(1, 16):
+            send_slot(block * 16 + lax.rem(s + j, 16))
+        return k
+
+    lax.fori_loop(1, DP // 16 + 1, fill, 0)
+    for i in range(1, DP // 16):
+        send_slot(lax.rem(s + 16 * i, DP))
     slot_in[s] = slot_out[s]
 
     some = pair_in.at[pl.ds(0, MP - 1)]
@@ -471,7 +510,7 @@
         result[...] = sums[:, 0:PART]
 
     for c in range(CH):
-        some = xall.at[c, pl.ds(0, MP - 1), pl.ds(0, XROWS if c == 0 else PART)]
+        some = xall.at[c, pl.ds(0, MP - 1)]
         to_mp(1, some, some, x_send.at[c], x_recv.at[c, 0]).wait_send()
         some = part_out.at[c, pl.ds(0, MP - 1)]
         to_mp(1, some, some, p_send.at[c], p_recv.at[c, 0]).wait_send()
@@ -530,7 +569,9 @@
             pltpu.VMEM((FULL, 128), F32),
             pltpu.VMEM((FFP, 128), F32),
             pltpu.VMEM((PART, 128), F32),
-            pltpu.VMEM((FFP, ROWS), BF16),
+            pltpu.VMEM((FULL, L), BF16),
+            pltpu.VMEM((CH, FFP, L), BF16),
+            pltpu.VMEM((CH, MP, PART, L), F32),
             pltpu.VMEM((CH, 7, PART, L), BF16),
             pltpu.VMEM((CH, 7, PART, L), BF16),
             pltpu.VMEM((MP, 24, 256), F32),
@@ -542,6 +583,7 @@
             pltpu.VMEM((MP, 32, SIDE), BF16),
             pltpu.VMEM((2, GROUP, IMG, 256), BF16),
             pltpu.VMEM((2, GROUP, IMG, 256), BF16),
+            pltpu.VMEM((ROWS, ROWS), BF16),
             pltpu.VMEM((2, DP * 16, ROWS), BF16),
             pltpu.VMEM((DP * 16, 128), BF16),
             pltpu.VMEM((2, DP * 16, SLOTS), BF16),

time: 67.8 us -> 72.1 us (1.063)
  Pallas kernels: 67 us -> 70.6 us
    pallas_call x1, Pallas kernels: 65.4 us -> 69 us  [shards(): pl.pallas_call(kernel, out_shape=shapes, in_specs=[hbm] * 10, out_specs=(...]
where the time goes in v3:
time: 72.1 us; the launch traced here: 71.2 us
  Pallas kernels  70.6 us (98%)
    pallas_call x1, Pallas kernels, shards(): pl.pallas_call(kernel, out_shape=shapes, in_specs=[hbm] * 10, out_specs=(...  69 us
    pallas_call x1, Pallas kernels, shards(): pl.pallas_call(hand_over, out_shape=shapes, in_specs=[vmem] * 3, out_spec...  1.63 us

profile of v3, /device:TPU:1, one launch (start us, length us, event | category | flops | bytes accessed | tf_op | source)
XLA Modules:
  0.0 71.2 jit_solution(6917403803989005184)
XLA Ops:
  0.6 69.0 %shard_map.121 = (bf16[144,640]{1,0:T(8,128)(2,1)}, f32[16,144]{1,0:T(8,128)}, f32[16,144]{1,0:T(8,128)}) custom-call(bf16[144,512]{1,0:T(8,128)(2,1)} %bitcast.8, bf16[16,144]{1,0:T(8,128)(2,1)} %text_hbm.1, s32[1,512]{1,0:T(1,128)} %bitcast.9, s32[1,512]{1,0:T(1,128)} %owner_hbm.1, s32[1,16]{1,0:T(1,128)} %bitcast.10, bf16[144]{0:T(256)(128)(2,1)} %gain_hbm.1, ...), custom_call_target="tpu_custom_call" | custom-call | tf_op jit(solution)/shard_map/pallas_call | solution.py:550
  69.6 1.6 %shard_map.122 = (bf16[144,640]{1,0:T(8,128)(2,1)}, f32[16,144]{1,0:T(8,128)}, f32[16,144]{1,0:T(8,128)}) custom-call(bf16[144,640]{1,0:T(8,128)(2,1)} %get-tuple-element.9.packed_in, f32[16,144]{1,0:T(8,128)} %get-tuple-element.10.image_in, f32[16,144]{1,0:T(8,128)} %get-tuple-element.11.text_in), custom_call_target="tpu_custom_call" | custom-call | tf_op jit(solution)/shard_map/pallas_call | solution.py:611

commit v4 on v2

--- a/solution.py
+++ b/solution.py
@@ -55,10 +55,10 @@
     packed_ref, image_grad_ref, text_grad_ref,
     x_ref, text_ref, target_ref, owner_ref, caption_ref, gain_ref, b1_ref, b2_ref, w1, w2,
     small_ref, w2t, xall, gain_b, b1_b, b2_b, hid, part_out, part_in,
-    pool_out, pool_in, tbuf, ibuf, pair_out, pair_in, coef_in, grad_out, grad_in,
+    pool_out, pool_in, tbuf, ibuf, pair_out, pair_in, grad_out, grad_in,
     pick, empty_pick, sel, rows_out, slot_out, slot_in,
     load_sem, x_send, x_recv, t_send, t_recv, p_send, p_recv,
-    pool_send, pool_recv, i_send, i_recv, pair_send, pair_recv, coef_send, coef_recv,
+    pool_send, pool_recv, i_send, i_recv, pair_send, pair_recv,
     grad_send, grad_recv, slot_send, slot_recv,
 ):
     s = lax.axis_index("dp")
@@ -222,8 +222,8 @@
         even_at = first + 2 * (slot - CAP)
         main_at = jnp.where(is_head, first + slot, jnp.where(is_tail, even_at, -1))
         odd_at = jnp.where(is_tail, even_at + 1, -1)
-        sel[0, lines, :] = jnp.where(main_at == column, 1.0, 0.0).astype(BF16)
-        sel[1, lines, :] = jnp.where(odd_at == column, 1.0, 0.0).astype(BF16)
+        here = jnp.logical_or(main_at == column, odd_at == column)
+        sel[lines, :] = jnp.where(here, 1.0, 0.0).astype(BF16)
         return k
 
     lax.fori_loop(0, DP * 16 // 128, build_pick, 0)
@@ -295,8 +295,8 @@
         there = lax.rem(m + i, MP)
         lines = pl.ds(pl.multiple_of(there * PART, 16), PART)
         got = nt(mixed, w2t[lines, :])
-        pool_out[there, 0:16, 0:PART] = got[0:16] + got[16:32]
-        pool_out[there, 16:24, 0:PART] = got[32:40]
+        pool_out[there, 0:16, 0:PART] = (got[0:16] + got[16:32]).astype(BF16)
+        pool_out[there, 16:32, 0:PART] = got[32:48].astype(BF16)
         return k
 
     pool_out[...] = jnp.zeros_like(pool_out)
@@ -315,9 +315,9 @@
 
     some = pool_in.at[pl.ds(0, MP - 1)]
     to_mp(1, some, some, pool_send.at[0], pool_recv.at[0]).wait_recv()
-    pooled = pool_in[0]
+    pooled = pool_in[0].astype(F32)
     for k in range(1, MP):
-        pooled = pooled + pool_in[k]
+        pooled = pooled + pool_in[k].astype(F32)
     b2_wide = jnp.where(iota((1, 256), 1) < PART, small_ref[2:3, 0:256], 0.0)
     counts = jnp.sum(member_f, axis=1, keepdims=True)
     own_sum = nt(member, x_ref[...])
@@ -344,28 +344,23 @@
     some = ibuf.at[pl.ds(0, GROUP - 1)]
     to_dp(neighbour, some, some, i_send.at[0], i_recv.at[0]).wait_recv()
     dots = nt(ibuf[...].reshape(SIDE, 256), tbuf[...].reshape(SIDE, 256))
-    feature = iota((1, 256), 1) < PART
-    image_f = jnp.where(feature, ibuf[...].reshape(SIDE, 256).astype(F32), 0.0)
-    image_sq = jnp.sum(image_f * image_f, axis=1, keepdims=True)
-    image_sq = jnp.where(iota((SIDE, SIDE), 1) == 0, image_sq, 0.0)
-    text_f = tbuf[...].reshape(SIDE, 256).astype(F32)
-    text_f = text_f * text_f
-    top = text_f.astype(BF16)
-    rest = (text_f - top.astype(F32)).astype(BF16)
-    ones = jnp.ones((16, 256), BF16)
-    text_sq = (nt(ones, top) + nt(ones, rest))[0:8]
-    for k in range(MP):
-        pair_out[k, 0:16] = dots[k * IMG : (k + 1) * IMG]
-        pair_out[k, 16:32] = image_sq[k * IMG : (k + 1) * IMG]
-        pair_out[k, 32:40] = text_sq
+    ones = jnp.where(iota((8, 256), 1) < PART, 1.0, 0.0).astype(BF16)
+
+    def squares(block):
+        value = block.astype(F32)
+        return nt(ones, (value * value).astype(BF16))
+
+    text_sq = squares(tbuf[...].reshape(SIDE, 256))
+    image_sq = squares(ibuf[...].reshape(SIDE, 256))
+    pair_out[0:SIDE] = dots.astype(BF16)
+    pair_out[SIDE : SIDE + 16] = jnp.concatenate([text_sq, image_sq], axis=0).astype(BF16)
 
     def send_pair(i, k):
-        there = lax.rem(m + i, MP)
-        to_mp(i, pair_out.at[there], pair_in.at[m], pair_send.at[0], pair_recv.at[0]).start()
+        to_mp(i, pair_out, pair_in.at[m], pair_send.at[0], pair_recv.at[0]).start()
         return k
 
     lax.fori_loop(1, MP, send_pair, 0, unroll=True)
-    pair_in[m] = pair_out[m]
+    pair_in[m] = pair_out[...]
 
 
     encoded = []
@@ -412,29 +407,21 @@
 
     some = pair_in.at[pl.ds(0, MP - 1)]
     to_mp(1, some, some, pair_send.at[0], pair_recv.at[0]).wait_recv()
-    total = pair_in[0]
+    total = pair_in[0].astype(F32)
     for k in range(1, MP):
-        total = total + pair_in[k]
-    image_scale = lax.rsqrt(total[16:32, 0:1] + 1e-06)
-    text_scale = lax.rsqrt(total[32:33] + 1e-06)
+        total = total + pair_in[k].astype(F32)
+    text_scale = lax.rsqrt(total[SIDE : SIDE + 1] + 1e-06)
+    image_row = lax.rsqrt(total[SIDE + 8 : SIDE + 9] + 1e-06)
+    image_scale = jnp.transpose(jnp.broadcast_to(image_row, (SIDE, SIDE)))
     place = iota((1, SIDE), 1)
     text_name = (jnp.right_shift(place, 4) * (GROUP * IMG) + b * IMG + jnp.bitwise_and(place, 15)).astype(F32)
-    noted = ibuf[m].astype(F32)
-    caption = noted[:, PART : PART + 1] * 32.0 + noted[:, PART + 1 : PART + 2]
-    logits = LOGIT_SCALE * (total[0:16] * image_scale * text_scale) + LOGIT_BIAS
+    noted = ibuf[...].reshape(SIDE, 256)[:, 128:256].astype(F32)
+    caption = noted[:, PART - 128 : PART - 127] * 32.0 + noted[:, PART - 127 : PART - 126]
+    logits = LOGIT_SCALE * (total[0:SIDE] * image_scale * text_scale) + LOGIT_BIAS
     coef = 1.0 / (1.0 + jnp.exp(-logits)) - jnp.where(caption == text_name, 1.0, 0.0)
-    coef_in[m] = jnp.concatenate([coef * text_scale, coef * image_scale], axis=0).astype(BF16)
-
-    def send_coef(i, k):
-        to_mp(i, coef_in.at[m], coef_in.at[m], coef_send.at[0], coef_recv.at[0]).start()
-        return k
-
-    lax.fori_loop(1, MP, send_coef, 0, unroll=True)
-    some = coef_in.at[pl.ds(0, MP - 1)]
-    to_mp(1, some, some, coef_send.at[0], coef_recv.at[0]).wait_recv()
-
-    for_images = jnp.concatenate([coef_in[k, 0:16] for k in range(MP)], axis=0)
-    for_texts = jnp.concatenate([coef_in[k, 16:32] for k in range(MP)], axis=0)
+    for_images = (coef * text_scale).astype(BF16)
+    for_texts = (coef * image_scale).astype(BF16)
+
     part = LOGIT_SCALE * nn(for_images, tbuf[...].reshape(SIDE, 256))
     grad_out[0] = part.astype(BF16).reshape(GROUP, IMG, 256)
     part = LOGIT_SCALE * tn(for_texts, ibuf[...].reshape(SIDE, 256))
@@ -455,12 +442,12 @@
     to_dp(neighbour, some, some, slot_send.at[0], slot_recv.at[0]).wait_recv()
     arrived = jnp.transpose(slot_in[...].reshape(DP * 16, 128))
     head_lane = jnp.bitwise_and(iota((1, DP * 16), 1), 15) < CAP
-    nothing = jnp.zeros((16, DP * 16), BF16)
-    main = jnp.concatenate([jnp.where(head_lane, arrived, 0), jnp.where(head_lane, nothing, arrived[0:16])], axis=0)
-    odd = jnp.where(head_lane, nothing, arrived[16:32])
-    placed = nn(main, sel[0])
+    nothing = jnp.zeros((32, DP * 16), BF16)
+    both = jnp.concatenate([jnp.where(head_lane, arrived, 0), jnp.where(head_lane, nothing, arrived[0:32])], axis=0)
+    placed = nn(both, sel[...])
+    even_slot = jnp.bitwise_and(iota((1, SLOTS), 1), 1) == 0
     packed_ref[0:128, :] = placed[0:128].astype(BF16)
-    packed_ref[128:PART, :] = (placed[128:PART] + nn(odd, sel[1])).astype(BF16)
+    packed_ref[128:PART, :] = jnp.where(even_slot, placed[128:PART], placed[PART : PART + 16]).astype(BF16)
 
     for n, result in enumerate((image_grad_ref, text_grad_ref)):
         some = grad_in.at[n, pl.ds(0, GROUP - 1)]
@@ -477,10 +464,8 @@
         to_mp(1, some, some, p_send.at[c], p_recv.at[c, 0]).wait_send()
     some = pool_out.at[pl.ds(0, MP - 1)]
     to_mp(1, some, some, pool_send.at[0], pool_recv.at[0]).wait_send()
-    some = pair_out.at[pl.ds(0, MP - 1)]
+    some = pair_in.at[pl.ds(0, MP - 1)]
     to_mp(1, some, some, pair_send.at[0], pair_recv.at[0]).wait_send()
-    some = coef_in.at[pl.ds(0, MP - 1)]
-    to_mp(1, some, some, coef_send.at[0], coef_recv.at[0]).wait_send()
     for buf, send, recv in (
         (tbuf, t_send.at[0], t_recv.at[0]),
         (ibuf, i_send.at[0], i_recv.at[0]),
@@ -533,18 +518,17 @@
             pltpu.VMEM((FFP, ROWS), BF16),
             pltpu.VMEM((CH, 7, PART, L), BF16),
             pltpu.VMEM((CH, 7, PART, L), BF16),
-            pltpu.VMEM((MP, 24, 256), F32),
-            pltpu.VMEM((MP, 24, 256), F32),
+            pltpu.VMEM((MP, 32, 256), BF16),
+            pltpu.VMEM((MP, 32, 256), BF16),
             pltpu.VMEM((GROUP, IMG, 256), BF16),
             pltpu.VMEM((GROUP, IMG, 256), BF16),
-            pltpu.VMEM((MP, 40, SIDE), F32),
-            pltpu.VMEM((MP, 40, SIDE), F32),
-            pltpu.VMEM((MP, 32, SIDE), BF16),
+            pltpu.VMEM((SIDE + 16, SIDE), BF16),
+            pltpu.VMEM((MP, SIDE + 16, SIDE), BF16),
             pltpu.VMEM((2, GROUP, IMG, 256), BF16),
             pltpu.VMEM((2, GROUP, IMG, 256), BF16),
             pltpu.VMEM((2, DP * 16, ROWS), BF16),
             pltpu.VMEM((DP * 16, 128), BF16),
-            pltpu.VMEM((2, DP * 16, SLOTS), BF16),
+            pltpu.VMEM((DP * 16, SLOTS), BF16),
             pltpu.VMEM((ROWS, 384), BF16),
             pltpu.VMEM((DP, 16, 128), BF16),
             pltpu.VMEM((DP, 16, 128), BF16),
@@ -552,7 +536,6 @@
             dma((CH,)), dma((CH, 7)),
             dma((1,)), dma((1,)),
             dma((CH,)), dma((CH, 7)),
-            dma((1,)), dma((1,)),
             dma((1,)), dma((1,)),
             dma((1,)), dma((1,)),
             dma((1,)), dma((1,)),

time: 67.8 us -> 67.3 us (level)
  no operation moved by 1% of the time
where the time goes in v4:
time: 67.3 us; the launch traced here: 67.1 us
  Pallas kernels  66.5 us (99%)
    pallas_call x1, Pallas kernels, shards(): pl.pallas_call(kernel, out_shape=shapes, in_specs=[hbm] * 10, out_specs=(...  64.9 us
    pallas_call x1, Pallas kernels, shards(): pl.pallas_call(hand_over, out_shape=shapes, in_specs=[vmem] * 3, out_spec...  1.63 us

profile of v4, /device:TPU:1, one launch (start us, length us, event | category | flops | bytes accessed | tf_op | source)
XLA Modules:
  0.0 67.1 jit_solution(14544779728027087770)
XLA Ops:
  0.6 64.9 %shard_map.121 = (bf16[144,640]{1,0:T(8,128)(2,1)}, f32[16,144]{1,0:T(8,128)}, f32[16,144]{1,0:T(8,128)}) custom-call(bf16[144,512]{1,0:T(8,128)(2,1)} %bitcast.8, bf16[16,144]{1,0:T(8,128)(2,1)} %text_hbm.1, s32[1,512]{1,0:T(1,128)} %bitcast.9, s32[1,512]{1,0:T(1,128)} %owner_hbm.1, s32[1,16]{1,0:T(1,128)} %bitcast.10, bf16[144]{0:T(256)(128)(2,1)} %gain_hbm.1, ...), custom_call_target="tpu_custom_call" | custom-call | tf_op jit(solution)/shard_map/pallas_call | solution.py:496
  65.5 1.6 %shard_map.122 = (bf16[144,640]{1,0:T(8,128)(2,1)}, f32[16,144]{1,0:T(8,128)}, f32[16,144]{1,0:T(8,128)}) custom-call(bf16[144,640]{1,0:T(8,128)(2,1)} %get-tuple-element.9.packed_in, f32[16,144]{1,0:T(8,128)} %get-tuple-element.10.image_in, f32[16,144]{1,0:T(8,128)} %get-tuple-element.11.text_in), custom_call_target="tpu_custom_call" | custom-call | tf_op jit(solution)/shard_map/pallas_call | solution.py:552

commit v5 on v4

--- a/solution.py
+++ b/solution.py
@@ -283,6 +283,8 @@
             first_sums(c)
 
     first_sums(CH - 1)
+    second_sums(0)
+
     member_f = jnp.where(iota((IMG, ROWS), 0) == owner_ref[...], 1.0, 0.0)
     member = member_f.astype(BF16)
     sums = nt(member, hid[...])
@@ -310,8 +312,8 @@
     lax.fori_loop(1, MP, send_pool, 0, unroll=True)
     pool_in[m] = pool_out[m]
 
-    for c in range(CH):
-        second_sums(c)
+    second_sums(1)
+    third_sums(0)
 
     some = pool_in.at[pl.ds(0, MP - 1)]
     to_mp(1, some, some, pool_send.at[0], pool_recv.at[0]).wait_recv()
@@ -338,8 +340,16 @@
 
     lax.fori_loop(1, GROUP, send_image, 0, unroll=True)
 
-    for c in range(CH):
-        third_sums(c)
+    third_sums(1)
+
+    def finish(c):
+        total = share(c, m) + arrived_sum(c, 4) + arrived_sum(c, 5) + arrived_sum(c, 6)
+        encoded = x_ref[:, c * L : (c + 1) * L].astype(F32) + total + wide(b2_b[...])
+        by_row = jnp.transpose(jnp.concatenate([encoded, jnp.zeros((256 - PART, L), F32)], axis=0))
+        rows_out[c * L : (c + 1) * L, 0:256] = by_row.astype(BF16)
+        rows_out[c * L : (c + 1) * L, 256:384] = pltpu.roll(by_row[:, 128:256], 16, 1).astype(BF16)
+
+    finish(0)
 
     some = ibuf.at[pl.ds(0, GROUP - 1)]
     to_dp(neighbour, some, some, i_send.at[0], i_recv.at[0]).wait_recv()
@@ -363,15 +373,8 @@
     pair_in[m] = pair_out[...]
 
 
-    encoded = []
-    for c in range(CH):
-        total = share(c, m) + arrived_sum(c, 4) + arrived_sum(c, 5) + arrived_sum(c, 6)
-        own = x_ref[:, c * L : (c + 1) * L].astype(F32)
-        encoded.append(own + total + wide(b2_b[...]))
-    encoded = jnp.concatenate(encoded, axis=1)
-    by_row = jnp.transpose(jnp.concatenate([encoded, jnp.zeros((256 - PART, ROWS), F32)], axis=0))
-    rows_out[:, 0:256] = by_row.astype(BF16)
-    rows_out[:, 256:384] = pltpu.roll(by_row[:, 128:256], 16, 1).astype(BF16)
+    finish(1)
+
     empty_f = jnp.broadcast_to(empty.astype(F32), (128, 256))
     line = iota((128, 128), 0)
     empty_tail = empty_f[:, 128:256]

time: 67.3 us -> 68.2 us (1.013)
  Pallas kernels: 66.5 us -> 67.4 us
    pallas_call x1, Pallas kernels: 64.9 us -> 65.8 us  [shards(): pl.pallas_call(kernel, out_shape=shapes, in_specs=[hbm] * 10, out_specs=(...]
where the time goes in v5:
time: 68.2 us; the launch traced here: 68.1 us
  Pallas kernels  67.4 us (99%)
    pallas_call x1, Pallas kernels, shards(): pl.pallas_call(kernel, out_shape=shapes, in_specs=[hbm] * 10, out_specs=(...  65.8 us
    pallas_call x1, Pallas kernels, shards(): pl.pallas_call(hand_over, out_shape=shapes, in_specs=[vmem] * 3, out_spec...  1.63 us

profile of v5, /device:TPU:1, one launch (start us, length us, event | category | flops | bytes accessed | tf_op | source)
XLA Modules:
  0.0 68.1 jit_solution(12442390428735292832)
XLA Ops:
  0.6 65.8 %shard_map.121 = (bf16[144,640]{1,0:T(8,128)(2,1)}, f32[16,144]{1,0:T(8,128)}, f32[16,144]{1,0:T(8,128)}) custom-call(bf16[144,512]{1,0:T(8,128)(2,1)} %bitcast.8, bf16[16,144]{1,0:T(8,128)(2,1)} %text_hbm.1, s32[1,512]{1,0:T(1,128)} %bitcast.9, s32[1,512]{1,0:T(1,128)} %owner_hbm.1, s32[1,16]{1,0:T(1,128)} %bitcast.10, bf16[144]{0:T(256)(128)(2,1)} %gain_hbm.1, ...), custom_call_target="tpu_custom_call" | custom-call | tf_op jit(solution)/shard_map/pallas_call | solution.py:499
  66.4 1.6 %shard_map.122 = (bf16[144,640]{1,0:T(8,128)(2,1)}, f32[16,144]{1,0:T(8,128)}, f32[16,144]{1,0:T(8,128)}) custom-call(bf16[144,640]{1,0:T(8,128)(2,1)} %get-tuple-element.9.packed_in, f32[16,144]{1,0:T(8,128)} %get-tuple-element.10.image_in, f32[16,144]{1,0:T(8,128)} %get-tuple-element.11.text_in), custom_call_target="tpu_custom_call" | custom-call | tf_op jit(solution)/shard_map/pallas_call | solution.py:555

commit v6 on v4

--- a/solution.py
+++ b/solution.py
@@ -59,7 +59,7 @@
     pick, empty_pick, sel, rows_out, slot_out, slot_in,
     load_sem, x_send, x_recv, t_send, t_recv, p_send, p_recv,
     pool_send, pool_recv, i_send, i_recv, pair_send, pair_recv,
-    grad_send, grad_recv, slot_send, slot_recv,
+    grad_send, grad_recv, slot_send, slot_recv, ready_sem,
 ):
     s = lax.axis_index("dp")
     m = lax.axis_index("mp")
@@ -331,6 +331,13 @@
     some = tbuf.at[pl.ds(0, GROUP - 1)]
     to_dp(neighbour, some, some, t_send.at[0], t_recv.at[0]).wait_recv()
 
+    def tell(i, k):
+        peer = a * GROUP + lax.rem(b + i, GROUP)
+        pl.semaphore_signal(ready_sem, inc=1, device_id=(peer, m), device_id_type=MESH)
+        return k
+
+    lax.fori_loop(1, GROUP, tell, 0, unroll=True)
+
     def send_image(i, k):
         peer = a * GROUP + lax.rem(b + i, GROUP)
         to_dp(peer, ibuf.at[b], ibuf.at[b], i_send.at[0], i_recv.at[0]).start()
@@ -340,28 +347,6 @@
 
     for c in range(CH):
         third_sums(c)
-
-    some = ibuf.at[pl.ds(0, GROUP - 1)]
-    to_dp(neighbour, some, some, i_send.at[0], i_recv.at[0]).wait_recv()
-    dots = nt(ibuf[...].reshape(SIDE, 256), tbuf[...].reshape(SIDE, 256))
-    ones = jnp.where(iota((8, 256), 1) < PART, 1.0, 0.0).astype(BF16)
-
-    def squares(block):
-        value = block.astype(F32)
-        return nt(ones, (value * value).astype(BF16))
-
-    text_sq = squares(tbuf[...].reshape(SIDE, 256))
-    image_sq = squares(ibuf[...].reshape(SIDE, 256))
-    pair_out[0:SIDE] = dots.astype(BF16)
-    pair_out[SIDE : SIDE + 16] = jnp.concatenate([text_sq, image_sq], axis=0).astype(BF16)
-
-    def send_pair(i, k):
-        to_mp(i, pair_out, pair_in.at[m], pair_send.at[0], pair_recv.at[0]).start()
-        return k
-
-    lax.fori_loop(1, MP, send_pair, 0, unroll=True)
-    pair_in[m] = pair_out[...]
-
 
     encoded = []
     for c in range(CH):
@@ -399,7 +384,32 @@
             send_slot(block * 16 + j)
         return k
 
-    lax.fori_loop(1, DP // 16, fill_other, 0)
+    pl.semaphore_wait(ready_sem, GROUP - 1)
+    lax.fori_loop(1, 3, fill_other, 0)
+
+    some = ibuf.at[pl.ds(0, GROUP - 1)]
+    to_dp(neighbour, some, some, i_send.at[0], i_recv.at[0]).wait_recv()
+    dots = nt(ibuf[...].reshape(SIDE, 256), tbuf[...].reshape(SIDE, 256))
+    ones = jnp.where(iota((8, 256), 1) < PART, 1.0, 0.0).astype(BF16)
+
+    def squares(block):
+        value = block.astype(F32)
+        return nt(ones, (value * value).astype(BF16))
+
+    text_sq = squares(tbuf[...].reshape(SIDE, 256))
+    image_sq = squares(ibuf[...].reshape(SIDE, 256))
+    pair_out[0:SIDE] = dots.astype(BF16)
+    pair_out[SIDE : SIDE + 16] = jnp.concatenate([text_sq, image_sq], axis=0).astype(BF16)
+
+    def send_pair(i, k):
+        to_mp(i, pair_out, pair_in.at[m], pair_send.at[0], pair_recv.at[0]).start()
+        return k
+
+    lax.fori_loop(1, MP, send_pair, 0, unroll=True)
+    pair_in[m] = pair_out[...]
+
+
+    lax.fori_loop(3, DP // 16, fill_other, 0)
     fill(s // 16)
     for j in range(1, 16):
         send_slot(s // 16 * 16 + lax.rem(s + j, 16))
@@ -541,6 +551,7 @@
             dma((1,)), dma((1,)),
             dma((2,)), dma((2,)),
             dma((1,)), dma((1,)),
+            pltpu.SemaphoreType.REGULAR,
         ],
         compiler_params=pltpu.CompilerParams(
             collective_id=0, has_side_effects=True, vmem_limit_bytes=60 * 1024 * 1024

time: 67.3 us -> 66.1 us (0.982)
  Pallas kernels: 66.5 us -> 64.7 us
    pallas_call x1, Pallas kernels: 64.9 us -> 63 us  [shards(): pl.pallas_call(kernel, out_shape=shapes, in_specs=[hbm] * 10, out_specs=(...]
where the time goes in v6:
time: 66.1 us; the launch traced here: 65.3 us
  Pallas kernels  64.7 us (98%)
    pallas_call x1, Pallas kernels, shards(): pl.pallas_call(kernel, out_shape=shapes, in_specs=[hbm] * 10, out_specs=(...  63 us
    pallas_call x1, Pallas kernels, shards(): pl.pallas_call(hand_over, out_shape=shapes, in_specs=[vmem] * 3, out_spec...  1.63 us

profile of v6, /device:TPU:1, one launch (start us, length us, event | category | flops | bytes accessed | tf_op | source)
XLA Modules:
  0.0 65.3 jit_solution(9830711337369888278)
XLA Ops:
  0.6 63.0 %shard_map.121 = (bf16[144,640]{1,0:T(8,128)(2,1)}, f32[16,144]{1,0:T(8,128)}, f32[16,144]{1,0:T(8,128)}) custom-call(bf16[144,512]{1,0:T(8,128)(2,1)} %bitcast.8, bf16[16,144]{1,0:T(8,128)(2,1)} %text_hbm.1, s32[1,512]{1,0:T(1,128)} %bitcast.9, s32[1,512]{1,0:T(1,128)} %owner_hbm.1, s32[1,16]{1,0:T(1,128)} %bitcast.10, bf16[144]{0:T(256)(128)(2,1)} %gain_hbm.1, ...), custom_call_target="tpu_custom_call" | custom-call | tf_op jit(solution)/shard_map/pallas_call | solution.py:506
  63.7 1.6 %shard_map.122 = (bf16[144,640]{1,0:T(8,128)(2,1)}, f32[16,144]{1,0:T(8,128)}, f32[16,144]{1,0:T(8,128)}) custom-call(bf16[144,640]{1,0:T(8,128)(2,1)} %get-tuple-element.9.packed_in, f32[16,144]{1,0:T(8,128)} %get-tuple-element.10.image_in, f32[16,144]{1,0:T(8,128)} %get-tuple-element.11.text_in), custom_call_target="tpu_custom_call" | custom-call | tf_op jit(solution)/shard_map/pallas_call | solution.py:563

commit v7 on v6

--- a/solution.py
+++ b/solution.py
@@ -283,6 +283,8 @@
             first_sums(c)
 
     first_sums(CH - 1)
+    second_sums(0)
+
     member_f = jnp.where(iota((IMG, ROWS), 0) == owner_ref[...], 1.0, 0.0)
     member = member_f.astype(BF16)
     sums = nt(member, hid[...])
@@ -310,8 +312,8 @@
     lax.fori_loop(1, MP, send_pool, 0, unroll=True)
     pool_in[m] = pool_out[m]
 
-    for c in range(CH):
-        second_sums(c)
+    second_sums(1)
+    third_sums(0)
 
     some = pool_in.at[pl.ds(0, MP - 1)]
     to_mp(1, some, some, pool_send.at[0], pool_recv.at[0]).wait_recv()
@@ -345,18 +347,19 @@
 
     lax.fori_loop(1, GROUP, send_image, 0, unroll=True)
 
-    for c in range(CH):
-        third_sums(c)
-
-    encoded = []
-    for c in range(CH):
+    third_sums(1)
+
+    def finish(c):
         total = share(c, m) + arrived_sum(c, 4) + arrived_sum(c, 5) + arrived_sum(c, 6)
-        own = x_ref[:, c * L : (c + 1) * L].astype(F32)
-        encoded.append(own + total + wide(b2_b[...]))
-    encoded = jnp.concatenate(encoded, axis=1)
-    by_row = jnp.transpose(jnp.concatenate([encoded, jnp.zeros((256 - PART, ROWS), F32)], axis=0))
-    rows_out[:, 0:256] = by_row.astype(BF16)
-    rows_out[:, 256:384] = pltpu.roll(by_row[:, 128:256], 16, 1).astype(BF16)
+        encoded = x_ref[:, c * L : (c + 1) * L].astype(F32) + total + wide(b2_b[...])
+        by_row = jnp.transpose(jnp.concatenate([encoded, jnp.zeros((256 - PART, L), F32)], axis=0))
+        rows_out[c * L : (c + 1) * L, 0:256] = by_row.astype(BF16)
+        rows_out[c * L : (c + 1) * L, 256:384] = pltpu.roll(by_row[:, 128:256], 16, 1).astype(BF16)
+
+    for c in range(CH):
+        finish(c)
+
+
     empty_f = jnp.broadcast_to(empty.astype(F32), (128, 256))
     line = iota((128, 128), 0)
     empty_tail = empty_f[:, 128:256]

time: 66.1 us -> 67 us (1.014)
  Pallas kernels: 64.7 us -> 66.2 us
    pallas_call x1, Pallas kernels: 63 us -> 64.6 us  [shards(): pl.pallas_call(kernel, out_shape=shapes, in_specs=[hbm] * 10, out_specs=(...]
where the time goes in v7:
time: 67 us; the launch traced here: 66.8 us
  Pallas kernels  66.2 us (99%)
    pallas_call x1, Pallas kernels, shards(): pl.pallas_call(kernel, out_shape=shapes, in_specs=[hbm] * 10, out_specs=(...  64.6 us
    pallas_call x1, Pallas kernels, shards(): pl.pallas_call(hand_over, out_shape=shapes, in_specs=[vmem] * 3, out_spec...  1.63 us

profile of v7, /device:TPU:1, one launch (start us, length us, event | category | flops | bytes accessed | tf_op | source)
XLA Modules:
  0.0 66.8 jit_solution(2260411869656239422)
XLA Ops:
  0.6 64.6 %shard_map.121 = (bf16[144,640]{1,0:T(8,128)(2,1)}, f32[16,144]{1,0:T(8,128)}, f32[16,144]{1,0:T(8,128)}) custom-call(bf16[144,512]{1,0:T(8,128)(2,1)} %bitcast.8, bf16[16,144]{1,0:T(8,128)(2,1)} %text_hbm.1, s32[1,512]{1,0:T(1,128)} %bitcast.9, s32[1,512]{1,0:T(1,128)} %owner_hbm.1, s32[1,16]{1,0:T(1,128)} %bitcast.10, bf16[144]{0:T(256)(128)(2,1)} %gain_hbm.1, ...), custom_call_target="tpu_custom_call" | custom-call | tf_op jit(solution)/shard_map/pallas_call | solution.py:509
  65.2 1.6 %shard_map.122 = (bf16[144,640]{1,0:T(8,128)(2,1)}, f32[16,144]{1,0:T(8,128)}, f32[16,144]{1,0:T(8,128)}) custom-call(bf16[144,640]{1,0:T(8,128)(2,1)} %get-tuple-element.9.packed_in, f32[16,144]{1,0:T(8,128)} %get-tuple-element.10.image_in, f32[16,144]{1,0:T(8,128)} %get-tuple-element.11.text_in), custom_call_target="tpu_custom_call" | custom-call | tf_op jit(solution)/shard_map/pallas_call | solution.py:566

commit v8 on v6

--- a/solution.py
+++ b/solution.py
@@ -385,7 +385,7 @@
         return k
 
     pl.semaphore_wait(ready_sem, GROUP - 1)
-    lax.fori_loop(1, 3, fill_other, 0)
+    lax.fori_loop(1, 2, fill_other, 0)
 
     some = ibuf.at[pl.ds(0, GROUP - 1)]
     to_dp(neighbour, some, some, i_send.at[0], i_recv.at[0]).wait_recv()
@@ -409,7 +409,7 @@
     pair_in[m] = pair_out[...]
 
 
-    lax.fori_loop(3, DP // 16, fill_other, 0)
+    lax.fori_loop(2, DP // 16, fill_other, 0)
     fill(s // 16)
     for j in range(1, 16):
         send_slot(s // 16 * 16 + lax.rem(s + j, 16))

time: 66.1 us -> 65.7 us (level)
  no operation moved by 1% of the time
where the time goes in v8:
time: 65.7 us; the launch traced here: 65.6 us
  Pallas kernels  64.9 us (99%)
    pallas_call x1, Pallas kernels, shards(): pl.pallas_call(kernel, out_shape=shapes, in_specs=[hbm] * 10, out_specs=(...  63.3 us
    pallas_call x1, Pallas kernels, shards(): pl.pallas_call(hand_over, out_shape=shapes, in_specs=[vmem] * 3, out_spec...  1.63 us

profile of v8, /device:TPU:1, one launch (start us, length us, event | category | flops | bytes accessed | tf_op | source)
XLA Modules:
  0.0 65.6 jit_solution(338716606835131714)
XLA Ops:
  0.6 63.3 %shard_map.121 = (bf16[144,640]{1,0:T(8,128)(2,1)}, f32[16,144]{1,0:T(8,128)}, f32[16,144]{1,0:T(8,128)}) custom-call(bf16[144,512]{1,0:T(8,128)(2,1)} %bitcast.8, bf16[16,144]{1,0:T(8,128)(2,1)} %text_hbm.1, s32[1,512]{1,0:T(1,128)} %bitcast.9, s32[1,512]{1,0:T(1,128)} %owner_hbm.1, s32[1,16]{1,0:T(1,128)} %bitcast.10, bf16[144]{0:T(256)(128)(2,1)} %gain_hbm.1, ...), custom_call_target="tpu_custom_call" | custom-call | tf_op jit(solution)/shard_map/pallas_call | solution.py:506
  63.9 1.6 %shard_map.122 = (bf16[144,640]{1,0:T(8,128)(2,1)}, f32[16,144]{1,0:T(8,128)}, f32[16,144]{1,0:T(8,128)}) custom-call(bf16[144,640]{1,0:T(8,128)(2,1)} %get-tuple-element.9.packed_in, f32[16,144]{1,0:T(8,128)} %get-tuple-element.10.image_in, f32[16,144]{1,0:T(8,128)} %get-tuple-element.11.text_in), custom_call_target="tpu_custom_call" | custom-call | tf_op jit(solution)/shard_map/pallas_call | solution.py:563

commit v9 on v8

--- a/solution.py
+++ b/solution.py
@@ -54,7 +54,7 @@
     x_hbm, text_hbm, target_hbm, owner_hbm, caption_hbm, gain_hbm, b1_hbm, b2_hbm, w1_hbm, w2_hbm,
     packed_ref, image_grad_ref, text_grad_ref,
     x_ref, text_ref, target_ref, owner_ref, caption_ref, gain_ref, b1_ref, b2_ref, w1, w2,
-    small_ref, w2t, xall, gain_b, b1_b, b2_b, hid, part_out, part_in,
+    small_ref, w2t, xall, gain_b, b1_b, b2_b, hid, own_ref, part_out, part_in,
     pool_out, pool_in, tbuf, ibuf, pair_out, pair_in, grad_out, grad_in,
     pick, empty_pick, sel, rows_out, slot_out, slot_in,
     load_sem, x_send, x_recv, t_send, t_recv, p_send, p_recv,
@@ -313,30 +313,31 @@
     for c in range(CH):
         second_sums(c)
 
+    some = tbuf.at[pl.ds(0, GROUP - 1)]
+    to_dp(neighbour, some, some, t_send.at[0], t_recv.at[0]).wait_recv()
+
+    def tell(i, k):
+        peer = a * GROUP + lax.rem(b + i, GROUP)
+        pl.semaphore_signal(ready_sem, inc=1, device_id=(peer, m), device_id_type=MESH)
+        return k
+
+    lax.fori_loop(1, GROUP, tell, 0, unroll=True)
+
+    counts = jnp.sum(member_f, axis=1, keepdims=True)
+    own_sum = nt(member, x_ref[...])
+    own_ref[...] = jnp.concatenate([own_sum, jnp.zeros((IMG, 256 - PART), F32)], axis=1)
+
     some = pool_in.at[pl.ds(0, MP - 1)]
     to_mp(1, some, some, pool_send.at[0], pool_recv.at[0]).wait_recv()
     pooled = pool_in[0].astype(F32)
     for k in range(1, MP):
         pooled = pooled + pool_in[k].astype(F32)
     b2_wide = jnp.where(iota((1, 256), 1) < PART, small_ref[2:3, 0:256], 0.0)
-    counts = jnp.sum(member_f, axis=1, keepdims=True)
-    own_sum = nt(member, x_ref[...])
-    own_sum = jnp.concatenate([own_sum, jnp.zeros((IMG, 256 - PART), F32)], axis=1)
-    image_own = (pooled[0:16] + own_sum) / counts + b2_wide
+    image_own = (pooled[0:16] + own_ref[...]) / counts + b2_wide
     empty = (pooled[16:17] + b2_wide).astype(BF16)
     lane = iota((IMG, 256), 1)
     image_note = jnp.where(lane == PART, as_column(caption_high), jnp.where(lane == PART + 1, as_column(caption_low), image_own))
     ibuf[b] = image_note.astype(BF16)
-
-    some = tbuf.at[pl.ds(0, GROUP - 1)]
-    to_dp(neighbour, some, some, t_send.at[0], t_recv.at[0]).wait_recv()
-
-    def tell(i, k):
-        peer = a * GROUP + lax.rem(b + i, GROUP)
-        pl.semaphore_signal(ready_sem, inc=1, device_id=(peer, m), device_id_type=MESH)
-        return k
-
-    lax.fori_loop(1, GROUP, tell, 0, unroll=True)
 
     def send_image(i, k):
         peer = a * GROUP + lax.rem(b + i, GROUP)
@@ -526,6 +527,7 @@
             pltpu.VMEM((FFP, 128), F32),
             pltpu.VMEM((PART, 128), F32),
             pltpu.VMEM((FFP, ROWS), BF16),
+            pltpu.VMEM((IMG, 256), F32),
             pltpu.VMEM((CH, 7, PART, L), BF16),
             pltpu.VMEM((CH, 7, PART, L), BF16),
             pltpu.VMEM((MP, 32, 256), BF16),

time: 65.7 us -> 66.2 us (level)
  no operation moved by 1% of the time
where the time goes in v9:
time: 66.2 us; the launch traced here: 65.4 us
  Pallas kernels  64.8 us (98%)
    pallas_call x1, Pallas kernels, shards(): pl.pallas_call(kernel, out_shape=shapes, in_specs=[hbm] * 10, out_specs=(...  63.1 us
    pallas_call x1, Pallas kernels, shards(): pl.pallas_call(hand_over, out_shape=shapes, in_specs=[vmem] * 3, out_spec...  1.63 us

profile of v9, /device:TPU:1, one launch (start us, length us, event | category | flops | bytes accessed | tf_op | source)
XLA Modules:
  0.0 65.4 jit_solution(11968857802707129401)
XLA Ops:
  0.6 63.1 %shard_map.121 = (bf16[144,640]{1,0:T(8,128)(2,1)}, f32[16,144]{1,0:T(8,128)}, f32[16,144]{1,0:T(8,128)}) custom-call(bf16[144,512]{1,0:T(8,128)(2,1)} %bitcast.8, bf16[16,144]{1,0:T(8,128)(2,1)} %text_hbm.1, s32[1,512]{1,0:T(1,128)} %bitcast.9, s32[1,512]{1,0:T(1,128)} %owner_hbm.1, s32[1,16]{1,0:T(1,128)} %bitcast.10, bf16[144]{0:T(256)(128)(2,1)} %gain_hbm.1, ...), custom_call_target="tpu_custom_call" | custom-call | tf_op jit(solution)/shard_map/pallas_call | solution.py:507
  63.8 1.6 %shard_map.122 = (bf16[144,640]{1,0:T(8,128)(2,1)}, f32[16,144]{1,0:T(8,128)}, f32[16,144]{1,0:T(8,128)}) custom-call(bf16[144,640]{1,0:T(8,128)(2,1)} %get-tuple-element.9.packed_in, f32[16,144]{1,0:T(8,128)} %get-tuple-element.10.image_in, f32[16,144]{1,0:T(8,128)} %get-tuple-element.11.text_in), custom_call_target="tpu_custom_call" | custom-call | tf_op jit(solution)/shard_map/pallas_call | solution.py:565
